TPU v7x, 256 devices: a whole 4x4x8 slice. The times are simulated.
256 devices in a mesh: layer: 8 (over z), plane: 32 (over y, x, core).
Axes of the slice: x: 4, y: 4, z: 8, core: 2. Of those that a mesh axis runs over, the one named last changes fastest.
Arguments:
- leaf_rhs: bfloat16 [2048, 128, 512], P(('layer', 'plane')), may hold values from -6 to 6
- leaf_inverse: bfloat16 [2048, 128, 128], P(('layer', 'plane')), may hold values from -0.5 to 0.5
- leaf_couple: bfloat16 [2048, 3, 1024, 128], P(('layer', 'plane')), may hold values from -0.09375 to 0.09375
- couple_mask: int32 [2048, 3], P(('layer', 'plane')), may hold values 0 or 1
- leaf_diag: float32 [2048, 128], P(('layer', 'plane')), may hold values from 0.5 to 2
- sep_rhs: bfloat16 [7, 1024, 512], P(None, 'plane'), may hold values from -6 to 6
- sep_inverse: bfloat16 [7, 1024, 1024], P(None, 'plane'), may hold values from -0.1875 to 0.1875
- sep_couple: bfloat16 [7, 2, 1024, 1024], P(None, None, 'plane'), may hold values from -0.125 to 0.125
- sep_diag: float32 [7, 1024], P(None, 'plane'), may hold values from 0.5 to 2
Outputs:
- leaf_solution: bfloat16 [2048, 128, 512], P(('layer', 'plane'))
- sep_solution: bfloat16 [8, 3, 1024, 512], P('layer', None, 'plane')
All inputs are finite; a program needn't handle non-finite values. No bound on the sum of `couple_mask` on one device may be relied on, other than what follows from the above.
Results may differ from a plain program's by a relative error of at most 0.02.
Values may be sent and summed in bfloat16 or wider, within the bound.
A program may use at most 128 MiB of HBM per device.

v0:
```python
import jax
import jax.numpy as jnp
from jax import lax
from jax.sharding import PartitionSpec as P


def from_partner(value, axis, stride):
    mask = 2**stride
    pairs = [(source, source ^ mask) for source in range(lax.axis_size(axis))]
    return lax.ppermute(value, axis, pairs)


def lower_unit(block, first_row):
    row_count = block.shape[-2]
    col_count = block.shape[-1]
    row_ids = first_row + lax.broadcasted_iota(jnp.int32, (row_count, col_count), 0)
    col_ids = lax.broadcasted_iota(jnp.int32, (row_count, col_count), 1)
    below = jnp.where(col_ids < row_ids, block, jnp.zeros_like(block))
    return jnp.where(col_ids == row_ids, jnp.ones_like(block), below)


def body(
    leaf_rhs,
    leaf_inverse,
    leaf_couple,
    couple_mask,
    leaf_diag,
    sep_rhs,
    sep_inverse,
    sep_couple,
    sep_diag,
):
    levels = leaf_couple.shape[1]
    layers = lax.axis_size("layer")
    own_rows = sep_rhs.shape[1]
    layer_id = lax.axis_index("layer")
    plane_id = lax.axis_index("plane")
    first_row = plane_id * own_rows
    leaf_lower = lower_unit(leaf_inverse, 0)
    leaf_y = jnp.einsum(
        "bij,bjr->bir", leaf_lower, leaf_rhs, preferred_element_type=jnp.float32
    ).astype(jnp.bfloat16)
    masked = leaf_couple * couple_mask.astype(jnp.bfloat16)[:, :, None, None]
    totals = lax.psum_scatter(
        jnp.einsum("bksc,bcr->skr", masked, leaf_y, preferred_element_type=jnp.float32),
        "plane",
        scatter_dimension=0,
        tiled=True,
    )
    sep_ids = [
        layers - (layers >> level - 1) + jnp.right_shift(layer_id, level)
        for level in range(1, levels + 1)
    ]

    def select_sep(array, level):
        return lax.dynamic_index_in_dim(array, sep_ids[level - 1], 0, keepdims=False)

    inverses = [
        lower_unit(select_sep(sep_inverse, level), first_row) for level in range(1, levels + 1)
    ]
    sep_z = []
    for level in range(1, levels + 1):
        partner = from_partner(totals[:, level - 1 :], "layer", level - 1)
        totals = jnp.concatenate([totals[:, : level - 1], totals[:, level - 1 :] + partner], axis=1)
        residual = (select_sep(sep_rhs, level).astype(jnp.float32) - totals[:, level - 1]).astype(
            jnp.bfloat16
        )
        residual_full = lax.all_gather(residual, "plane", axis=0, tiled=True)
        solved = jnp.dot(
            inverses[level - 1], residual_full, preferred_element_type=jnp.float32
        ).astype(jnp.bfloat16)
        if level < levels:
            solved_full = lax.all_gather(solved, "plane", axis=0, tiled=True)
        if level < levels:
            blocks = select_sep(sep_couple, level)[: levels - level]
            coupling = jnp.einsum(
                "jos,sr->ojr", blocks, solved_full, preferred_element_type=jnp.float32
            )
            totals = jnp.concatenate([totals[:, :level], totals[:, level:] + coupling], axis=1)
        sep_z.append(solved.astype(jnp.float32) / select_sep(sep_diag, level)[:, None])
    answers = [None] * levels
    for level in range(levels, 0, -1):
        if level < levels:
            blocks = select_sep(sep_couple, level)[: levels - level]
            upper_rows = jnp.stack(answers[level:])

            def couple_back(offset_row, row_count, blocks=blocks, upper_rows=upper_rows):
                return jnp.einsum(
                    "jos,jor->sr", blocks, upper_rows, preferred_element_type=jnp.float32
                )

            carried = lax.psum_scatter(
                couple_back(jnp.int32(0), lax.axis_size("plane") * own_rows),
                "plane",
                scatter_dimension=0,
                tiled=True,
            )
            target_now = (sep_z[level - 1] - carried).astype(jnp.bfloat16)
        else:
            target_now = sep_z[level - 1].astype(jnp.bfloat16)
        lower_part = inverses[level - 1]

        def transpose_solve(offset_row, row_count, lower_part=lower_part, target_now=target_now):
            return lax.dot_general(
                lower_part, target_now, (((0,), (0,)), ((), ())), preferred_element_type=jnp.float32
            )

        answers[level - 1] = lax.psum_scatter(
            transpose_solve(jnp.int32(0), lax.axis_size("plane") * own_rows),
            "plane",
            scatter_dimension=0,
            tiled=True,
        ).astype(jnp.bfloat16)
    above = lax.all_gather(jnp.stack(answers), "plane", axis=1, tiled=True)
    back_terms = jnp.einsum("bksc,ksr->bcr", masked, above, preferred_element_type=jnp.float32)
    leaf_target = (leaf_y.astype(jnp.float32) / leaf_diag[:, :, None] - back_terms).astype(
        jnp.bfloat16
    )
    leaf_solution = jnp.einsum(
        "bjc,bjr->bcr", leaf_lower, leaf_target, preferred_element_type=jnp.float32
    ).astype(jnp.bfloat16)
    sep_solution = jnp.stack(answers)[None]
    return (leaf_solution, sep_solution)


def solution(mesh):
    in_specs = (
        P(("layer", "plane"), None, None),
        P(("layer", "plane"), None, None),
        P(("layer", "plane"), None, None, None),
        P(("layer", "plane"), None),
        P(("layer", "plane"), None),
        P(None, "plane", None),
        P(None, "plane", None),
        P(None, None, "plane", None),
        P(None, "plane"),
    )
    out_specs = (P(("layer", "plane"), None, None), P("layer", None, "plane", None))
    return jax.shard_map(body, mesh=mesh, in_specs=in_specs, out_specs=out_specs, check_vma=False)
```

profile of v0, /device:TPU:1, one launch (start us, length us, event | category | flops | bytes accessed | tf_op | source)
XLA Modules:
  0.0 960.2 jit_solution(12969961117015314941)
XLA Ops:
  9.8 8.7 fusion.7
  18.5 9.5 copy.23
  29.8 132.8 %all-reduce.3.cloned.1.call-done = f32[1024,3,512]{2,1,0:T(4,128)} async-done(((f32[1024,3,512]{2,1,0:T(4,128)}), f32[1024,3,512]{2,1,0:T(4,128)}) %all-reduce.3.cloned.1.call-update) | async-done | bytes 6291472
  165.1 4.3 collective-permute-done
  170.9 49.2 %all-gather.7.cloned.1.call-done = bf16[1024,512]{1,0:T(8,128)(2,1)} async-done(((bf16[32,512]{1,0:T(8,128)(2,1)}), bf16[1024,512]{1,0:T(8,128)(2,1)}) %all-gather.7.cloned.1.call-update) | async-done | bytes 1048592 | tf_op jit(solution)/shard_map/all_gather | solution.py:68
  222.3 48.4 %all-gather.9.cloned.1.call-done = bf16[1024,512]{1,0:T(8,128)(2,1)} async-done(((bf16[32,512]{1,0:T(8,128)(2,1)}), bf16[1024,512]{1,0:T(8,128)(2,1)}) %all-gather.9.cloned.1.call-update) | async-done | bytes 1048592 | tf_op jit(solution)/shard_map/all_gather | solution.py:73
  272.3 2.3 collective-permute-start.1
  274.6 6.3 collective-permute-done.1
  282.4 48.1 %all-gather.11.cloned.1.call-done = bf16[1024,512]{1,0:T(8,128)(2,1)} async-done(((bf16[32,512]{1,0:T(8,128)(2,1)}), bf16[1024,512]{1,0:T(8,128)(2,1)}) %all-gather.11.cloned.1.call-update) | async-done | bytes 1048592 | tf_op jit(solution)/shard_map/all_gather | solution.py:68
  332.7 48.3 %all-gather.13.cloned.1.call-done = bf16[1024,512]{1,0:T(8,128)(2,1)} async-done(((bf16[32,512]{1,0:T(8,128)(2,1)}), bf16[1024,512]{1,0:T(8,128)(2,1)}) %all-gather.13.cloned.1.call-update) | async-done | bytes 1048592 | tf_op jit(solution)/shard_map/all_gather | solution.py:73
  382.5 5.5 collective-permute-start.2
  392.4 48.5 %all-gather.15.cloned.1.call-done = bf16[1024,512]{1,0:T(8,128)(2,1)} async-done(((bf16[32,512]{1,0:T(8,128)(2,1)}), bf16[1024,512]{1,0:T(8,128)(2,1)}) %all-gather.15.cloned.1.call-update) | async-done | bytes 1048592 | tf_op jit(solution)/shard_map/all_gather | solution.py:68
  440.9 3.3 fusion.28
  444.3 84.7 %reduce-scatter.6.cloned.1.call-done = f32[32,512]{1,0:T(8,128)} async-done(((f32[1024,512]{1,0:T(8,128)}), f32[32,512]{1,0:T(8,128)}) %reduce-scatter.6.cloned.1.call-update) | async-done | bytes 65552 | tf_op jit(solution)/shard_map/reduce_scatter | solution.py:108
  529.0 2.7 fusion.68
  531.8 87.4 %reduce-scatter.8.cloned.1.call-done = f32[32,512]{1,0:T(8,128)} async-done(((f32[1024,512]{1,0:T(8,128)}), f32[32,512]{1,0:T(8,128)}) %reduce-scatter.8.cloned.1.call-update) | async-done | bytes 65552 | tf_op jit(solution)/shard_map/reduce_scatter | solution.py:92
  619.2 2.7 fusion.69
  622.0 87.4 %reduce-scatter.10.cloned.1.call-done = f32[32,512]{1,0:T(8,128)} async-done(((f32[1024,512]{1,0:T(8,128)}), f32[32,512]{1,0:T(8,128)}) %reduce-scatter.10.cloned.1.call-update) | async-done | bytes 65552 | tf_op jit(solution)/shard_map/reduce_scatter | solution.py:108
  710.3 2.7 convolution_bitcast_fusion
  713.1 86.4 %reduce-scatter.12.cloned.1.call-done = f32[32,512]{1,0:T(8,128)} async-done(((f32[1024,512]{1,0:T(8,128)}), f32[32,512]{1,0:T(8,128)}) %reduce-scatter.12.cloned.1.call-update) | async-done | bytes 65552 | tf_op jit(solution)/shard_map/reduce_scatter | solution.py:92
  799.5 2.7 fusion.70
  802.3 87.4 %reduce-scatter.14.cloned.1.call-done = f32[32,512]{1,0:T(8,128)} async-done(((f32[1024,512]{1,0:T(8,128)}), f32[32,512]{1,0:T(8,128)}) %reduce-scatter.14.cloned.1.call-update) | async-done | bytes 65552 | tf_op jit(solution)/shard_map/reduce_scatter | solution.py:108
  891.3 53.4 %all-gather.17.cloned.1.call-done = bf16[3,1024,512]{2,1,0:T(8,128)(2,1)} async-done(((bf16[3,32,512]{2,1,0:T(8,128)(2,1)}), bf16[3,1024,512]{2,1,0:T(8,128)(2,1)}) %all-gather.17.cloned.1.call-update) | async-done | bytes 3145744 | tf_op jit(solution)/shard_map/all_gather | solution.py:114
  944.8 8.6 fusion.20
  (64 shorter events, 23.8 us)
Async XLA Ops:
  7.2 1.2 copy-start
  7.2 155.5 %all-reduce.3.cloned.1.call-start = ((), (), s32[]{:S(2)}) async-start(), calls=%async_computation.16 | async-start | bytes 16777216
  27.9 0.7 copy-start.7
  27.9 192.1 %copy-start.1 = (bf16[7,32,1024]{2,1,0:T(8,128)(2,1)S(1)}, bf16[7,32,1024]{2,1,0:T(8,128)(2,1)}, u32[]{:S(2)}) copy-start(bf16[7,32,1024]{2,1,0:T(8,128)(2,1)} %param.15) | copy-start | bytes 1376260
  28.0 192.1 %all-gather.7.cloned.1.call-start = ((), (), s32[]{:S(2)}) async-start(), calls=%async_computation.5 | async-start | bytes 1081344 | tf_op jit(solution)/shard_map/all_gather | solution.py:68
  163.7 5.6 collective-permute-start
  170.8 99.9 %all-gather.9.cloned.1.call-start = ((), (), s32[]{:S(2)}) async-start(), calls=%async_computation.6 | async-start | bytes 1081344 | tf_op jit(solution)/shard_map/all_gather | solution.py:73
  222.2 108.2 %all-gather.11.cloned.1.call-start = ((), (), s32[]{:S(2)}) async-start(), calls=%async_computation.7 | async-start | bytes 1081344 | tf_op jit(solution)/shard_map/all_gather | solution.py:68
  272.3 8.7 collective-permute-start.1
  282.4 98.7 %all-gather.13.cloned.1.call-start = ((), (), s32[]{:S(2)}) async-start(), calls=%async_computation.8 | async-start | bytes 1081344 | tf_op jit(solution)/shard_map/all_gather | solution.py:73
  332.7 108.2 %all-gather.15.cloned.1.call-start = ((), (), s32[]{:S(2)}) async-start(), calls=%async_computation.9 | async-start | bytes 1081344 | tf_op jit(solution)/shard_map/all_gather | solution.py:68
  382.5 7.6 collective-permute-start.2
  391.6 137.5 %reduce-scatter.6.cloned.1.call-start = ((), (), s32[]{:S(2)}) async-start(), calls=%async_computation.10 | async-start | bytes 2162688 | tf_op jit(solution)/shard_map/reduce_scatter | solution.py:108
  444.2 175.0 %copy-start.3 = (bf16[32,512]{1,0:T(8,128)(2,1)S(1)}, bf16[32,512]{1,0:T(8,128)(2,1)}, u32[]{:S(2)}) copy-start(bf16[32,512]{1,0:T(8,128)(2,1)} %convolution_convert_fusion.2) | copy-start | bytes 98308
  444.2 175.0 %reduce-scatter.8.cloned.1.call-start = ((), (), s32[]{:S(2)}) async-start(), calls=%async_computation.11 | async-start | bytes 2162688 | tf_op jit(solution)/shard_map/reduce_scatter | solution.py:92
  531.7 90.3 %copy-start.5 = (f32[32,512]{1,0:T(8,128)S(1)}, f32[32,512]{1,0:T(8,128)}, u32[]{:S(2)}) copy-start(f32[32,512]{1,0:T(8,128)} %reduce-scatter.6.cloned.1.call-done) | copy-start | bytes 196612
  531.7 177.7 %reduce-scatter.10.cloned.1.call-start = ((), (), s32[]{:S(2)}) async-start(), calls=%async_computation.12 | async-start | bytes 2162688 | tf_op jit(solution)/shard_map/reduce_scatter | solution.py:108
  621.9 177.6 %copy-start.2 = (bf16[32,512]{1,0:T(8,128)(2,1)S(1)}, bf16[32,512]{1,0:T(8,128)(2,1)}, u32[]{:S(2)}) copy-start(bf16[32,512]{1,0:T(8,128)(2,1)} %convolution_convert_fusion.3) | copy-start | bytes 98308
  622.0 177.6 %reduce-scatter.12.cloned.1.call-start = ((), (), s32[]{:S(2)}) async-start(), calls=%async_computation.13 | async-start | bytes 2162688 | tf_op jit(solution)/shard_map/reduce_scatter | solution.py:92
  713.0 231.7 %copy-start.4 = (bf16[8,128,128]{2,1,0:T(8,128)(2,1)S(1)}, bf16[8,128,128]{2,1,0:T(8,128)(2,1)}, u32[]{:S(2)}) copy-start(bf16[8,128,128]{2,1,0:T(8,128)(2,1)} %param.10) | copy-start | bytes 786436
  713.0 231.7 %copy-start.6 = (f32[8,128]{1,0:T(8,128)S(1)}, f32[8,128]{1,0:T(8,128)}, u32[]{:S(2)}) copy-start(f32[8,128]{1,0:T(8,128)} %param.13) | copy-start | bytes 12292
  713.1 176.7 %reduce-scatter.14.cloned.1.call-start = ((), (), s32[]{:S(2)}) async-start(), calls=%async_computation.14 | async-start | bytes 2162688 | tf_op jit(solution)/shard_map/reduce_scatter | solution.py:108
  802.3 142.5 %all-gather.17.cloned.1.call-start = ((), (), s32[]{:S(2)}) async-start(), calls=%async_computation.15 | async-start | bytes 3244032 | tf_op jit(solution)/shard_map/all_gather | solution.py:114
Sparse Core Ops, SparseCore 0:
  28.1 134.5 all-reduce.2
  171.0 49.0 all-gather.6
  223.5 47.1 all-gather.8
  282.5 47.9 all-gather.10
  333.8 47.1 all-gather.12
  391.7 49.1 all-gather.14
  445.2 83.7 reduce-scatter.5
  533.3 85.8 reduce-scatter.7
  623.5 85.8 reduce-scatter.9
  713.6 85.8 reduce-scatter.11
  803.9 85.8 reduce-scatter.13
  893.1 51.5 all-gather.16
where the time goes:
time: 961 us; the launch traced here: 960 us
  waiting for transfers between devices  875 us (91%)
  matrix products  40.2 us (4%)
  between operations  15 us (2%)
  local copies, waits for them, and re-layouts  12.9 us (1%)
  starting transfers between devices  9.71 us (1%)
    reduce_scatter x3, waiting for transfers between devices, body(): lax.psum_scatter(transpose_solve(jnp.int32(0), lax.axis_size('plane') * o...  260 us
    reduce_scatter x2, waiting for transfers between devices, body(): lax.psum_scatter(couple_back(jnp.int32(0), lax.axis_size('plane') * own_r...  174 us
    all_gather x3, waiting for transfers between devices, body(): residual_full = lax.all_gather(residual, 'plane', axis=0, tiled=True)  146 us
    unnamed x13, waiting for transfers between devices  133 us
    all_gather x2, waiting for transfers between devices, body(): solved_full = lax.all_gather(solved, 'plane', axis=0, tiled=True)  96.7 us
    all_gather x1, waiting for transfers between devices, body(): above = lax.all_gather(jnp.stack(answers), 'plane', axis=1, tiled=True)  53.4 us
  transfers between devices with their start and end apart: 15, of which 15 were waited for; matrix products, arithmetic and copies ran while one was open for 0% of the time, Pallas kernels for 0%

commit v1 on v0

v1 whole, which is shorter than its diff:
```python
import jax
import jax.numpy as jnp
from jax import lax
from jax.experimental import pallas as pl
from jax.experimental.pallas import tpu as pltpu
from jax.sharding import PartitionSpec as P

BF16 = jnp.bfloat16
F32 = jnp.float32
SIDE = 4
CORES = 2
EXTRA = 128
TILE = 256


def dot_rows(left, right):
    return lax.dot_general(left, right, (((1,), (1,)), ((), ())), preferred_element_type=F32)


def dot_cols(left, right):
    return lax.dot_general(left, right, (((1,), (0,)), ((), ())), preferred_element_type=F32)


def unit_lower(block, first_row):
    row_ids = first_row + lax.broadcasted_iota(jnp.int32, block.shape, 0)
    col_ids = lax.broadcasted_iota(jnp.int32, block.shape, 1)
    value = block.astype(F32)
    value = jnp.where(col_ids < row_ids, value, 0.0)
    return jnp.where(col_ids == row_ids, 1.0, value).astype(BF16)


def kernel(
    mask_ref,
    rhs_hbm,
    inverse_hbm,
    couple_hbm,
    diag_hbm,
    sep_rhs_hbm,
    sep_inverse_hbm,
    sep_couple_hbm,
    sep_diag_hbm,
    leaf_out,
    sep_out,
    rhs,
    inverse,
    couple,
    diag,
    sep_rhs,
    own_inverse,
    own_diag,
    mat0,
    mat1,
    mat2,
    leaf_y,
    leaf_ym,
    lower_t,
    part,
    paired,
    chip_sum,
    in1,
    sum1,
    in2,
    total,
    from_odd,
    out_total,
    to_two,
    from_one,
    to_three,
    from_two,
    sep_y,
    sep_z,
    answer,
    back,
    local_sem,
    couple_sem,
    g_send,
    g_recv,
    gc_send,
    gc_recv,
    r_send,
    r_recv,
    rc_send,
    rc_recv,
    a_send,
    a_recv,
    ac_send,
    ac_recv,
    odd_send,
    odd_recv,
    two_send,
    two_recv,
    three_send,
    three_recv,
    x_send,
    x_recv,
):
    blocks, blk, right_sides = rhs.shape
    own_rows = own_inverse.shape[0]
    size = own_inverse.shape[1]
    half = size // 2
    layer = lax.axis_index("layer")
    plane = lax.axis_index("plane")
    layers = lax.axis_size("layer")
    y = plane // (SIDE * CORES)
    x = (plane // CORES) % SIDE
    core = plane % CORES
    first_row = plane * own_rows

    def at_plane(y_at, x_at, core_at):
        return (layer, (y_at * SIDE + x_at) * CORES + core_at)

    def x_peer(d):
        return at_plane(y, (x + d) % SIDE, core)

    def y_peer(d):
        return at_plane((y + d) % SIDE, x, core)

    sibling = at_plane(y, x, 1 - core)

    is_one = layer % 2 == 0
    is_odd = layer % 2 == 1
    is_two = layer % 4 == 1
    is_three = layer == 3
    has_first = layer != 7
    has_second = jnp.logical_or(is_one, is_two)
    sep_of = [layer // 2, 4 + layer // 4, 6 + layer * 0]
    own_sep = jnp.where(is_one, layer // 2, jnp.where(is_two, 4 + layer // 4, 6))

    sends = []

    def remote(parts, when=None):
        def make():
            src, dst, send_sem, recv_sem, device = parts()
            return pltpu.make_async_remote_copy(
                src_ref=src,
                dst_ref=dst,
                send_sem=send_sem,
                recv_sem=recv_sem,
                device_id=device,
                device_id_type=pl.DeviceIdType.MESH,
            )

        make().start()
        sends.append((when, make))

    def arrived(dst, sem):
        pltpu.make_async_copy(dst, dst, sem).wait()

    barrier = pltpu.get_barrier_semaphore()
    peers = [sibling]
    for d in range(1, SIDE):
        peers += [x_peer(d), y_peer(d)]
    for d in range(1, 8):
        peers.append(((layer + d) % 8, plane))
    for peer in peers:
        pl.semaphore_signal(barrier, inc=1, device_id=peer, device_id_type=pl.DeviceIdType.MESH)

    local = [
        pltpu.make_async_copy(sep_inverse_hbm.at[own_sep], own_inverse, local_sem.at[0]),
        pltpu.make_async_copy(sep_diag_hbm, own_diag, local_sem.at[1]),
        pltpu.make_async_copy(sep_couple_hbm.at[own_sep, 0], mat1.at[y, x, core], local_sem.at[2]),
        pltpu.make_async_copy(sep_couple_hbm.at[own_sep, 1], mat2.at[y, x, core], local_sem.at[3]),
        pltpu.make_async_copy(inverse_hbm, inverse, local_sem.at[4]),
        pltpu.make_async_copy(rhs_hbm, rhs, local_sem.at[5]),
        pltpu.make_async_copy(diag_hbm, diag, local_sem.at[6]),
        pltpu.make_async_copy(sep_rhs_hbm.at[sep_of[0]], sep_rhs.at[0], local_sem.at[7]),
        pltpu.make_async_copy(sep_rhs_hbm.at[sep_of[1]], sep_rhs.at[1], local_sem.at[8]),
        pltpu.make_async_copy(sep_rhs_hbm.at[sep_of[2]], sep_rhs.at[2], local_sem.at[9]),
    ]
    for copy in local:
        copy.start()
    couples = []
    for k in range(3):
        couples.append(
            [
                pltpu.make_async_copy(
                    couple_hbm.at[b, k], couple.at[k, :, pl.ds(b * blk, blk)], couple_sem.at[k, b]
                )
                for b in range(blocks)
            ]
        )
        for copy in couples[k]:
            copy.start()

    def lanes(buf, h):
        return pl.ds(0, half) if h == 0 else pl.ds(half, buf().shape[-1] - half)

    def send_first(buf, sems, h, d, when):
        def parts():
            ref = buf().at[y, x, core, :, lanes(buf, h)]
            send, recv = sems(0, h, d - 1)
            return ref, ref, send, recv, x_peer(d) if h == 0 else y_peer(d)

        remote(parts, when)

    def send_second(buf, sems, h, d, when):
        def parts():
            if h == 0:
                ref = buf().at[y, :, core, :, lanes(buf, h)]
            else:
                ref = buf().at[:, x, core, :, lanes(buf, h)]
            send, recv = sems(1, h, d - 1)
            return ref, ref, send, recv, y_peer(d) if h == 0 else x_peer(d)

        remote(parts, when)

    def gather_first(buf, sems, when=None):
        for h in range(2):
            for d in range(1, SIDE):
                send_first(buf, sems, h, d, when)

    def gather_second(buf, sems, when=None):
        for h in range(2):
            for d in range(1, SIDE):
                if h == 0:
                    ref = buf().at[y, (x - d + SIDE) % SIDE, core, :, lanes(buf, h)]
                else:
                    ref = buf().at[(y - d + SIDE) % SIDE, x, core, :, lanes(buf, h)]
                arrived(ref, sems(0, h, d - 1)[1])
            for d in range(1, SIDE):
                send_second(buf, sems, h, d, when)

    def gather_third(buf, sems, c_sems, when=None):
        for h in range(2):
            for d in range(1, SIDE):
                if h == 0:
                    ref = buf().at[(y - d + SIDE) % SIDE, :, core, :, lanes(buf, h)]
                else:
                    ref = buf().at[:, (x - d + SIDE) % SIDE, core, :, lanes(buf, h)]
                arrived(ref, sems(1, h, d - 1)[1])

        def parts():
            ref = buf().at[:, :, core]
            return (ref, ref) + c_sems() + (sibling,)

        remote(parts, when)

    def gather_end(buf, c_recv):
        arrived(buf.at[:, :, 1 - core], c_recv)

    mats = [mat0, mat1, mat2]
    uses = [has_first, has_second, is_one]

    def whole(m):
        return mats[m][:, :, :, :, 0:size].reshape(size, size)

    def mat_parts(m):
        return (
            lambda: mats[m],
            lambda *at: (g_send.at[(m,) + at], g_recv.at[(m,) + at]),
            lambda: (gc_send.at[m], gc_recv.at[m]),
        )

    def mat_first(m):
        buf, sems, _ = mat_parts(m)

        @pl.when(uses[m])
        def _():
            gather_first(buf, sems, uses[m])

    def mat_second(m):
        buf, sems, _ = mat_parts(m)

        @pl.when(uses[m])
        def _():
            gather_second(buf, sems, uses[m])

    def mat_third(m):
        buf, sems, c_sems = mat_parts(m)

        @pl.when(uses[m])
        def _():
            gather_third(buf, sems, c_sems, uses[m])

    def mat_end(m):
        gather_end(mats[m], gc_recv.at[m])

    local[0].wait()
    local[1].wait()
    eye = lax.broadcasted_iota(jnp.int32, (own_rows, own_rows), 0) == lax.broadcasted_iota(
        jnp.int32, (own_rows, own_rows), 1
    )
    sep_rows = lax.broadcasted_iota(jnp.int32, own_diag.shape, 0) == own_sep
    diag_row = jnp.sum(jnp.where(sep_rows, own_diag[...], 0.0), axis=0, keepdims=True)
    diag_col = jnp.sum(jnp.where(eye, diag_row, 0.0), axis=1, keepdims=True)
    high = diag_col.astype(BF16).astype(F32)
    middle = (diag_col - high).astype(BF16).astype(F32)
    low = diag_col - high - middle
    lane = lax.broadcasted_iota(jnp.int32, (own_rows, EXTRA), 1)
    beside = jnp.where(
        lane == 0, high, jnp.where(lane == 1, middle, jnp.where(lane == 2, low, 0.0))
    ).astype(BF16)
    mat0[y, x, core, :, 0:size] = unit_lower(own_inverse[...], first_row)
    mat0[y, x, core, :, size:] = beside
    pl.semaphore_wait(barrier, len(peers))
    mat_first(0)
    local[2].wait()
    local[3].wait()
    mat_first(1)
    mat_first(2)

    for i in range(4, 10):
        local[i].wait()

    def solve_leaf(b, _):
        lower = unit_lower(inverse[b], 0)
        lower_t[b] = lower.astype(F32).T.astype(BF16)
        rhs_t = rhs[b].T
        columns = pl.ds(pl.multiple_of(b * blk, blk), blk)
        leaf_y[:, columns] = dot_rows(rhs_t, lower).astype(BF16)
        return 0

    lax.fori_loop(0, blocks, solve_leaf, 0)

    block_of = lax.broadcasted_iota(jnp.int32, (1, blocks * blk), 1) // blk

    def mask_lanes(k):
        result = jnp.zeros((1, blocks * blk), F32)
        for b in range(blocks):
            result = result + jnp.where(block_of == b, mask_ref[b, k].astype(F32), 0.0)
        return result

    def leaf_part(k):
        for copy in couples[k]:
            copy.wait()
        leaf_ym[...] = leaf_y[...] * mask_lanes(k).astype(BF16)
        rhs_t = sep_rhs[k].T
        adds = layer % (2 ** (k + 1)) == 0
        first = jnp.where(adds, first_row, size)

        def tile(i, _):
            start = pl.multiple_of(i * TILE, TILE)
            columns = pl.ds(start, TILE)
            rows_at = first + lax.broadcasted_iota(jnp.int32, (own_rows, TILE), 0)
            cols_at = start + lax.broadcasted_iota(jnp.int32, (own_rows, TILE), 1)
            place = jnp.where(rows_at == cols_at, 1.0, 0.0).astype(BF16)
            term = dot_cols(rhs_t, place) - dot_rows(leaf_ym[...], couple[k, columns, :])
            part[k, :, :, :, :, columns] = term.astype(BF16).reshape(
                part.shape[1:-1] + (TILE,)
            )
            return 0

        lax.fori_loop(0, size // TILE, tile, 0)
        remote(
            lambda: (
                part.at[k, :, :, 1 - core],
                paired.at[k],
                rc_send.at[k],
                rc_recv.at[k],
                sibling,
            )
        )

    def reduce_first(k):
        arrived(paired.at[k], rc_recv.at[k])
        chip_sum[k] = (part[k, :, :, core].astype(F32) + paired[k].astype(F32)).astype(BF16)
        for h in range(2):
            for d in range(1, SIDE):
                send_part(k, h, d)

    def send_part(k, h, d):
        def parts():
            if h == 0:
                ref = chip_sum.at[k, :, (x + d) % SIDE, :, pl.ds(0, half)]
            else:
                ref = chip_sum.at[k, (y + d) % SIDE, :, :, pl.ds(half, half)]
            return (
                ref,
                in1.at[k, h, d - 1],
                r_send.at[k, 0, h, d - 1],
                r_recv.at[k, 0, h, d - 1],
                x_peer(d) if h == 0 else y_peer(d),
            )

        remote(parts)

    def send_sum(k, h, d):
        remote(
            lambda: (
                sum1.at[k, h, ((y if h == 0 else x) + d) % SIDE],
                in2.at[k, h, d - 1],
                r_send.at[k, 1, h, d - 1],
                r_recv.at[k, 1, h, d - 1],
                y_peer(d) if h == 0 else x_peer(d),
            )
        )

    def reduce_second(k):
        for h in range(2):
            if h == 0:
                value = chip_sum[k, :, x, :, 0:half].astype(F32)
            else:
                value = chip_sum[k, y, :, :, half:].astype(F32)
            for d in range(1, SIDE):
                arrived(in1.at[k, h, d - 1], r_recv.at[k, 0, h, d - 1])
                value = value + in1[k, h, d - 1].astype(F32)
            sum1[k, h] = value.astype(BF16)
            for d in range(1, SIDE):
                send_sum(k, h, d)

    def reduce_end(k):
        for h in range(2):
            value = sum1[k, h, y if h == 0 else x].astype(F32)
            for d in range(1, SIDE):
                arrived(in2.at[k, h, d - 1], r_recv.at[k, 1, h, d - 1])
                value = value + in2[k, h, d - 1].astype(F32)
            total[k, :, h * half : (h + 1) * half] = value

        @pl.when(is_odd)
        def _():
            out_total[k] = total[k].astype(BF16)
            remote(
                lambda: (
                    out_total.at[k],
                    from_odd.at[k],
                    odd_send.at[k],
                    odd_recv.at[k],
                    ((layer + 7) % 8, plane),
                ),
                is_odd,
            )

    def whole_total(k):
        arrived(from_odd.at[k], odd_recv.at[k])
        return total[k] + from_odd[k].astype(F32)

    def divide(value):
        picks = jnp.where(
            lax.broadcasted_iota(jnp.int32, (value.shape[0], EXTRA), 1) < 3, 1.0, 0.0
        ).astype(BF16)
        parts = mat0[:, :, :, :, size:].reshape(size, EXTRA)
        return value / dot_rows(picks, parts)

    def forward(residual):
        solved = dot_rows(residual.astype(BF16), whole(0)).astype(BF16)
        sep_y[...] = solved
        sep_z[...] = divide(solved.astype(F32))

    two_of = (layer // 4) * 4 + 1
    two_slot = (layer % 4) // 2

    leaf_part(0)
    mat_second(0)
    leaf_part(1)
    reduce_first(0)
    leaf_part(2)
    mat_second(1)
    reduce_first(1)
    reduce_second(0)
    mat_third(0)
    reduce_first(2)
    reduce_end(0)
    reduce_second(1)

    @pl.when(is_one)
    def _():
        residual = whole_total(0)
        mat_end(0)
        forward(residual)

    mat_third(1)
    reduce_end(1)
    mat_second(2)
    reduce_second(2)

    def pass_up(k):
        to_two[k - 1] = (whole_total(k) - dot_rows(sep_y[...], whole(k))).astype(BF16)
        remote(
            lambda: (
                to_two.at[k - 1],
                from_one.at[two_slot, k - 1],
                two_send.at[k - 1],
                two_recv.at[two_slot, k - 1],
                (two_of, plane),
            ),
            is_one,
        )

    @pl.when(is_one)
    def _():
        mat_end(1)
        pass_up(1)

    reduce_end(2)
    mat_third(2)

    @pl.when(is_one)
    def _():
        mat_end(2)
        pass_up(2)

    @pl.when(is_two)
    def _():
        mat_end(0)
        mat_end(1)
        for slot in range(2):
            arrived(from_one.at[slot, 0], two_recv.at[slot, 0])
        forward(from_one[0, 0].astype(F32) + from_one[1, 0].astype(F32))
        term = dot_rows(sep_y[...], whole(1))
        for slot in range(2):
            arrived(from_one.at[slot, 1], two_recv.at[slot, 1])
        to_three[...] = (from_one[0, 1].astype(F32) + from_one[1, 1].astype(F32) - term).astype(
            BF16
        )
        remote(
            lambda: (
                to_three,
                from_two.at[layer // 4],
                three_send,
                three_recv.at[layer // 4],
                (3, plane),
            ),
            is_two,
        )

    def finish(k, target):
        answer[k, y, x, core] = dot_cols(target.astype(BF16), whole(0)).astype(BF16)

    def own_answer(k):
        return answer.at[k, y, x, core]

    def send_answer(k, slot, layer_to, when):
        remote(
            lambda: (
                own_answer(k),
                own_answer(k),
                x_send.at[slot],
                x_recv.at[k],
                (layer_to(), plane),
            ),
            when,
        )

    @pl.when(is_three)
    def _():
        mat_end(0)
        for slot in range(2):
            arrived(from_two.at[slot], three_recv.at[slot])
        forward(from_two[0].astype(F32) + from_two[1].astype(F32))
        finish(2, sep_z[...])
        for slot, layer_to in enumerate((1, 5, 2, 4, 0, 6, 7)):
            send_answer(2, slot, lambda layer_to=layer_to: layer_to, is_three)

    @pl.when(jnp.logical_not(is_three))
    def _():
        arrived(own_answer(2), x_recv.at[2])

    @pl.when(is_two)
    def _():
        finish(1, sep_z[...] - dot_cols(own_answer(2)[...], whole(1)))
        for slot, shift in enumerate((7, 1, 2)):
            send_answer(1, 7 + slot, lambda shift=shift: (layer + shift) % 8, is_two)

    def answer_parts(k):
        return (
            lambda: answer.at[k],
            lambda *at: (a_send.at[(k,) + at], a_recv.at[(k,) + at]),
            lambda: (ac_send.at[k], ac_recv.at[k]),
        )

    def answer_first(k, when=None):
        gather_first(*answer_parts(k)[:2], when)

    def answer_second(k):
        gather_second(*answer_parts(k)[:2])

    def answer_third(k):
        gather_third(*answer_parts(k))

    def answer_whole(k):
        return answer[k].reshape(right_sides, size)

    answer_first(2)

    @pl.when(is_one)
    def _():
        sep_z[...] = sep_z[...] - dot_cols(own_answer(2)[...], whole(2))

    answer_second(2)

    @pl.when(jnp.logical_not(is_two))
    def _():
        arrived(own_answer(1), x_recv.at[1])

    @pl.when(is_one)
    def _():
        finish(0, sep_z[...] - dot_cols(own_answer(1)[...], whole(1)))
        send_answer(0, 10, lambda: layer + 1, is_one)
        answer_first(0, is_one)

    own_rows_at = jnp.where(
        first_row + lax.broadcasted_iota(jnp.int32, (own_rows, size), 0)
        == lax.broadcasted_iota(jnp.int32, (own_rows, size), 1),
        1.0,
        0.0,
    ).astype(BF16)

    def leaf_back(k):
        gather_end(answer.at[k], ac_recv.at[k])
        masks = mask_lanes(k)
        sep_out[0, k] = dot_rows(own_rows_at, answer_whole(k)).astype(BF16)
        leaf_ym[...] = jnp.broadcast_to(masks, leaf_ym.shape).astype(BF16)

        def tile(i, _):
            columns = pl.ds(pl.multiple_of(i * TILE, TILE), TILE)
            term = dot_cols(answer_whole(k), couple[k, :, columns]) * leaf_ym[
                :, columns
            ].astype(F32)
            back[:, columns] = term if k == 2 else back[:, columns] + term
            return 0

        lax.fori_loop(0, size // TILE, tile, 0)

    answer_first(1)
    answer_third(2)

    @pl.when(is_odd)
    def _():
        arrived(own_answer(0), x_recv.at[0])
        answer_first(0, is_odd)

    leaf_back(2)
    answer_second(1)
    answer_second(0)
    answer_third(1)
    leaf_back(1)
    answer_third(0)
    leaf_back(0)

    def solve_back(b, _):
        columns = pl.ds(pl.multiple_of(b * blk, blk), blk)
        target = leaf_y[:, columns].astype(F32) / diag[pl.ds(b, 1), :] - back[:, columns]
        leaf_out[b] = dot_rows(lower_t[b], target.astype(BF16)).astype(BF16)
        return 0

    lax.fori_loop(0, blocks, solve_back, 0)

    for when, make in sends:
        if when is None:
            make().wait_send()
    for group in (has_first, has_second, is_one, is_odd, is_two, is_three):

        @pl.when(group)
        def _(group=group):
            for when, make in sends:
                if when is group:
                    make().wait_send()


def body(
    leaf_rhs,
    leaf_inverse,
    leaf_couple,
    couple_mask,
    leaf_diag,
    sep_rhs,
    sep_inverse,
    sep_couple,
    sep_diag,
):
    blocks, levels, size, blk = leaf_couple.shape
    right_sides = leaf_rhs.shape[2]
    own_rows = sep_rhs.shape[1]
    cols = right_sides // (SIDE * SIDE * CORES)
    half = size // 2
    grid = (SIDE, SIDE, CORES)
    vmem = pltpu.VMEM
    dma = pltpu.SemaphoreType.DMA
    hops = (levels, 2, 2, SIDE - 1)
    scratch = [
        vmem(leaf_rhs.shape, BF16),
        vmem(leaf_inverse.shape, BF16),
        vmem((levels, size, blocks * blk), BF16),
        vmem(leaf_diag.shape, F32),
        vmem((levels, own_rows, right_sides), BF16),
        vmem((own_rows, size), BF16),
        vmem(sep_diag.shape, F32),
        vmem(grid + (own_rows, size + EXTRA), BF16),
        vmem(grid + (own_rows, size), BF16),
        vmem(grid + (own_rows, size), BF16),
        vmem((right_sides, blocks * blk), BF16),
        vmem((right_sides, blocks * blk), BF16),
        vmem(leaf_inverse.shape, BF16),
        vmem((levels,) + grid + (cols, size), BF16),
        vmem((levels, SIDE, SIDE, cols, size), BF16),
        vmem((levels, SIDE, SIDE, cols, size), BF16),
        vmem((levels, 2, SIDE - 1, SIDE, cols, half), BF16),
        vmem((levels, 2, SIDE, cols, half), BF16),
        vmem((levels, 2, SIDE - 1, cols, half), BF16),
        vmem((levels, cols, size), F32),
        vmem((levels, cols, size), BF16),
        vmem((levels, cols, size), BF16),
        vmem((2, cols, size), BF16),
        vmem((2, 2, cols, size), BF16),
        vmem((cols, size), BF16),
        vmem((2, cols, size), BF16),
        vmem((cols, size), BF16),
        vmem((cols, size), F32),
        vmem((levels,) + grid + (cols, size), BF16),
        vmem((right_sides, blocks * blk), F32),
        dma((10,)),
        dma((levels, blocks)),
        dma(hops),
        dma(hops),
        dma((levels,)),
        dma((levels,)),
        dma(hops),
        dma(hops),
        dma((levels,)),
        dma((levels,)),
        dma(hops),
        dma(hops),
        dma((levels,)),
        dma((levels,)),
        dma((levels,)),
        dma((levels,)),
        dma((2,)),
        dma((2, 2)),
        dma,
        dma((2,)),
        dma((11,)),
        dma((levels,)),
    ]
    any_space = pl.BlockSpec(memory_space=pl.ANY)
    in_vmem = pl.BlockSpec(memory_space=pltpu.VMEM)
    return pl.pallas_call(
        kernel,
        out_shape=(
            jax.ShapeDtypeStruct(leaf_rhs.shape, BF16),
            jax.ShapeDtypeStruct((1, levels, own_rows, right_sides), BF16),
        ),
        in_specs=[pl.BlockSpec(memory_space=pltpu.SMEM)] + [any_space] * 8,
        out_specs=(in_vmem, in_vmem),
        scratch_shapes=scratch,
        compiler_params=pltpu.CompilerParams(
            collective_id=0, has_side_effects=True, vmem_limit_bytes=56 * 2**20
        ),
    )(
        couple_mask,
        leaf_rhs,
        leaf_inverse,
        leaf_couple,
        leaf_diag,
        sep_rhs,
        sep_inverse,
        sep_couple,
        sep_diag,
    )


def solution(mesh):
    in_specs = (
        P(("layer", "plane"), None, None),
        P(("layer", "plane"), None, None),
        P(("layer", "plane"), None, None, None),
        P(("layer", "plane"), None),
        P(("layer", "plane"), None),
        P(None, "plane", None),
        P(None, "plane", None),
        P(None, None, "plane", None),
        P(None, "plane"),
    )
    out_specs = (P(("layer", "plane"), None, None), P("layer", None, "plane", None))
    return jax.shard_map(body, mesh=mesh, in_specs=in_specs, out_specs=out_specs, check_vma=False)
```

time: 961 us -> 102 us (0.11)
  waiting for transfers between devices: 875 us -> 0 us
  Pallas kernels: 0 us -> 95.8 us
  matrix products: 40.2 us -> 0 us
  between operations: 15 us -> 0.64 us
  starting transfers between devices: 9.71 us -> 0 us
    reduce_scatter x5 -> x0, waiting for transfers between devices: 433 us -> none  [the longest x3 260 us: body(): lax.psum_scatter(transpose_solve(jnp.int32(0), lax.axis_size('plane') * o...]
    all_gather x6 -> x0, waiting for transfers between devices: 296 us -> none  [the longest x3 146 us: body(): residual_full = lax.all_gather(residual, 'plane', axis=0, tiled=True)]
    unnamed x13 -> x0, waiting for transfers between devices: 133 us -> none
    pallas_call x0 -> x1, Pallas kernels: none -> 95.8 us  [body(): pl.pallas_call(kernel, out_shape=(jax.ShapeDtypeStruct(leaf_rhs.shape, BF...]
    dot_general x12 -> x0, matrix products: 40.2 us -> none  [the longest x3 8.76 us: transpose_solve(): lax.dot_general(lower_part, target_now, (((0,), (0,)), ((), ())), preferr...]
    ppermute x3 -> x0, waiting for transfers between devices: 12.7 us -> none  [from_partner(): return lax.ppermute(value, axis, pairs)]
  transfers between devices with their start and end apart: 15 -> 0, of which waited for: 15 -> 0; matrix products, arithmetic and copies ran while one was open for 0% -> 0% of each run, Pallas kernels for 0% -> 0%
where the time goes in v1:
time: 102 us
  Pallas kernels  95.8 us (94%)
  local copies, waits for them, and re-layouts  5.15 us (5%)
    pallas_call x1, Pallas kernels, body(): pl.pallas_call(kernel, out_shape=(jax.ShapeDtypeStruct(leaf_rhs.shape, BF...  95.8 us
    unnamed x3, local copies, waits for them, and re-layouts  5.15 us

profile of v1, /device:TPU:1, one launch (start us, length us, event | category | flops | bytes accessed | tf_op | source)
XLA Modules:
  0.0 101.6 jit_solution(8616716685965844348)
XLA Ops:
  0.6 1.3 %copy.11.mask_ref = s32[8,3]{1,0:T(8,128)} copy(s32[8,3]{0,1:T(4,128)} %param.12) | data formatting | bytes 192 | tf_op args[3]
  2.0 95.8 %shard_map.104 = (bf16[8,128,512]{2,1,0:T(8,128)(2,1)}, bf16[1,3,32,512]{3,2,1,0:T(8,128)(2,1)}) custom-call(s32[8,3]{1,0:T(8,128)} %copy.11.mask_ref, bf16[8,128,512]{2,1,0:T(8,128)(2,1)} %rhs_hbm.1, bf16[8,128,128]{2,1,0:T(8,128)(2,1)} %inverse_hbm.1, bf16[8,3,1024,128]{3,2,1,0:T(8,128)(2,1)} %couple_hbm.1, f32[8,128]{1,0:T(8,128)} %diag_hbm.1, ...), custom_call_target="tpu_custom_call" | custom-call | tf_op jit(solution)/shard_map/pallas_call | solution.py:726
  97.8 2.3 %copy.14 = bf16[8,128,512]{2,1,0:T(8,128)(2,1)} copy(bf16[8,128,512]{2,1,0:T(8,128)(2,1)} %get-tuple-element.4) | data formatting | bytes 2097152
  100.0 1.5 %copy.15 = bf16[1,3,32,512]{3,2,1,0:T(8,128)(2,1)} copy(bf16[1,3,32,512]{3,2,1,0:T(8,128)(2,1)} %get-tuple-element.5) | data formatting | bytes 196608

commit v2 on v1

--- a/solution.py
+++ b/solution.py
@@ -182,61 +182,64 @@
         for copy in couples[k]:
             copy.start()
 
-    def lanes(buf, h):
-        return pl.ds(0, half) if h == 0 else pl.ds(half, buf().shape[-1] - half)
-
-    def send_first(buf, sems, h, d, when):
+    def send_first(pick, width, sems, h, d, when):
         def parts():
-            ref = buf().at[y, x, core, :, lanes(buf, h)]
+            ref = pick(y, x, core, lanes(width, h))
             send, recv = sems(0, h, d - 1)
             return ref, ref, send, recv, x_peer(d) if h == 0 else y_peer(d)
 
         remote(parts, when)
 
-    def send_second(buf, sems, h, d, when):
+    def send_second(pick, width, sems, h, d, when):
         def parts():
+            everywhere = slice(None)
             if h == 0:
-                ref = buf().at[y, :, core, :, lanes(buf, h)]
+                ref = pick(y, everywhere, core, lanes(width, h))
             else:
-                ref = buf().at[:, x, core, :, lanes(buf, h)]
+                ref = pick(everywhere, x, core, lanes(width, h))
             send, recv = sems(1, h, d - 1)
             return ref, ref, send, recv, y_peer(d) if h == 0 else x_peer(d)
 
         remote(parts, when)
 
-    def gather_first(buf, sems, when=None):
+    def lanes(width, h):
+        return pl.ds(0, half) if h == 0 else pl.ds(half, width - half)
+
+    def gather_first(pick, width, sems, when=None):
         for h in range(2):
             for d in range(1, SIDE):
-                send_first(buf, sems, h, d, when)
-
-    def gather_second(buf, sems, when=None):
+                send_first(pick, width, sems, h, d, when)
+
+    def gather_second(pick, width, sems, when=None):
         for h in range(2):
             for d in range(1, SIDE):
                 if h == 0:
-                    ref = buf().at[y, (x - d + SIDE) % SIDE, core, :, lanes(buf, h)]
+                    ref = pick(y, (x - d + SIDE) % SIDE, core, lanes(width, h))
                 else:
-                    ref = buf().at[(y - d + SIDE) % SIDE, x, core, :, lanes(buf, h)]
+                    ref = pick((y - d + SIDE) % SIDE, x, core, lanes(width, h))
                 arrived(ref, sems(0, h, d - 1)[1])
             for d in range(1, SIDE):
-                send_second(buf, sems, h, d, when)
-
-    def gather_third(buf, sems, c_sems, when=None):
+                send_second(pick, width, sems, h, d, when)
+
+    def gather_third(pick, width, sems, c_sems, when=None):
+        everywhere = slice(None)
         for h in range(2):
             for d in range(1, SIDE):
                 if h == 0:
-                    ref = buf().at[(y - d + SIDE) % SIDE, :, core, :, lanes(buf, h)]
+                    ref = pick((y - d + SIDE) % SIDE, everywhere, core, lanes(width, h))
                 else:
-                    ref = buf().at[:, (x - d + SIDE) % SIDE, core, :, lanes(buf, h)]
+                    ref = pick(everywhere, (x - d + SIDE) % SIDE, core, lanes(width, h))
                 arrived(ref, sems(1, h, d - 1)[1])
 
         def parts():
-            ref = buf().at[:, :, core]
+            ref = pick(everywhere, everywhere, core, everywhere)
             return (ref, ref) + c_sems() + (sibling,)
 
         remote(parts, when)
 
-    def gather_end(buf, c_recv):
-        arrived(buf.at[:, :, 1 - core], c_recv)
+    def gather_end(pick, c_recv):
+        everywhere = slice(None)
+        arrived(pick(everywhere, everywhere, 1 - core, everywhere), c_recv)
 
     mats = [mat0, mat1, mat2]
     uses = [has_first, has_second, is_one]
@@ -246,34 +249,29 @@
 
     def mat_parts(m):
         return (
-            lambda: mats[m],
+            lambda y_at, x_at, core_at, at: mats[m].at[y_at, x_at, core_at, :, at],
+            mats[m].shape[-1],
             lambda *at: (g_send.at[(m,) + at], g_recv.at[(m,) + at]),
             lambda: (gc_send.at[m], gc_recv.at[m]),
         )
 
     def mat_first(m):
-        buf, sems, _ = mat_parts(m)
-
         @pl.when(uses[m])
         def _():
-            gather_first(buf, sems, uses[m])
+            gather_first(*mat_parts(m)[:3], uses[m])
 
     def mat_second(m):
-        buf, sems, _ = mat_parts(m)
-
         @pl.when(uses[m])
         def _():
-            gather_second(buf, sems, uses[m])
+            gather_second(*mat_parts(m)[:3], uses[m])
 
     def mat_third(m):
-        buf, sems, c_sems = mat_parts(m)
-
         @pl.when(uses[m])
         def _():
-            gather_third(buf, sems, c_sems, uses[m])
+            gather_third(*mat_parts(m), uses[m])
 
     def mat_end(m):
-        gather_end(mats[m], gc_recv.at[m])
+        gather_end(mat_parts(m)[0], gc_recv.at[m])
 
     local[0].wait()
     local[1].wait()
@@ -292,13 +290,6 @@
     ).astype(BF16)
     mat0[y, x, core, :, 0:size] = unit_lower(own_inverse[...], first_row)
     mat0[y, x, core, :, size:] = beside
-    pl.semaphore_wait(barrier, len(peers))
-    mat_first(0)
-    local[2].wait()
-    local[3].wait()
-    mat_first(1)
-    mat_first(2)
-
     for i in range(4, 10):
         local[i].wait()
 
@@ -312,12 +303,19 @@
 
     lax.fori_loop(0, blocks, solve_leaf, 0)
 
+    pl.semaphore_wait(barrier, len(peers))
+    mat_first(0)
+    local[2].wait()
+    local[3].wait()
+    mat_first(1)
+    mat_first(2)
+
     block_of = lax.broadcasted_iota(jnp.int32, (1, blocks * blk), 1) // blk
 
     def mask_lanes(k):
         result = jnp.zeros((1, blocks * blk), F32)
         for b in range(blocks):
-            result = result + jnp.where(block_of == b, mask_ref[b, k].astype(F32), 0.0)
+            result = result + jnp.where(block_of == b, mask_ref[k, b].astype(F32), 0.0)
         return result
 
     def leaf_part(k):
@@ -343,7 +341,7 @@
         lax.fori_loop(0, size // TILE, tile, 0)
         remote(
             lambda: (
-                part.at[k, :, :, 1 - core],
+                part.at[k, 1 - core],
                 paired.at[k],
                 rc_send.at[k],
                 rc_recv.at[k],
@@ -353,7 +351,7 @@
 
     def reduce_first(k):
         arrived(paired.at[k], rc_recv.at[k])
-        chip_sum[k] = (part[k, :, :, core].astype(F32) + paired[k].astype(F32)).astype(BF16)
+        chip_sum[k] = (part[k, core].astype(F32) + paired[k].astype(F32)).astype(BF16)
         for h in range(2):
             for d in range(1, SIDE):
                 send_part(k, h, d)
@@ -440,17 +438,17 @@
     two_slot = (layer % 4) // 2
 
     leaf_part(0)
-    mat_second(0)
     leaf_part(1)
     reduce_first(0)
+    mat_second(0)
     leaf_part(2)
+    reduce_first(1)
     mat_second(1)
-    reduce_first(1)
     reduce_second(0)
     mat_third(0)
-    reduce_first(2)
     reduce_end(0)
     reduce_second(1)
+    mat_second(2)
 
     @pl.when(is_one)
     def _():
@@ -458,9 +456,9 @@
         mat_end(0)
         forward(residual)
 
+    reduce_first(2)
+    reduce_end(1)
     mat_third(1)
-    reduce_end(1)
-    mat_second(2)
     reduce_second(2)
 
     def pass_up(k):
@@ -514,10 +512,10 @@
         )
 
     def finish(k, target):
-        answer[k, y, x, core] = dot_cols(target.astype(BF16), whole(0)).astype(BF16)
+        answer[k, core, y, x] = dot_cols(target.astype(BF16), whole(0)).astype(BF16)
 
     def own_answer(k):
-        return answer.at[k, y, x, core]
+        return answer.at[k, core, y, x]
 
     def send_answer(k, slot, layer_to, when):
         remote(
@@ -553,22 +551,23 @@
 
     def answer_parts(k):
         return (
-            lambda: answer.at[k],
+            lambda y_at, x_at, core_at, at: answer.at[k, core_at, y_at, x_at, :, at],
+            size,
             lambda *at: (a_send.at[(k,) + at], a_recv.at[(k,) + at]),
             lambda: (ac_send.at[k], ac_recv.at[k]),
         )
 
     def answer_first(k, when=None):
-        gather_first(*answer_parts(k)[:2], when)
+        gather_first(*answer_parts(k)[:3], when)
 
     def answer_second(k):
-        gather_second(*answer_parts(k)[:2])
+        gather_second(*answer_parts(k)[:3])
 
     def answer_third(k):
         gather_third(*answer_parts(k))
 
-    def answer_whole(k):
-        return answer[k].reshape(right_sides, size)
+    def answer_end(k):
+        gather_end(answer_parts(k)[0], ac_recv.at[k])
 
     answer_first(2)
 
@@ -595,18 +594,41 @@
         0.0,
     ).astype(BF16)
 
+    side_cols = right_sides // CORES
+
+    def rows_out(k, side):
+        value = dot_rows(own_rows_at, answer[k, side].reshape(side_cols, size)).astype(BF16)
+        sep_out[0, k, :, pl.ds(pl.multiple_of(side * side_cols, side_cols), side_cols)] = value
+
     def leaf_back(k):
-        gather_end(answer.at[k], ac_recv.at[k])
-        masks = mask_lanes(k)
-        sep_out[0, k] = dot_rows(own_rows_at, answer_whole(k)).astype(BF16)
-        leaf_ym[...] = jnp.broadcast_to(masks, leaf_ym.shape).astype(BF16)
+        answer_end(k)
+        rows_out(k, core)
+        rows_out(k, 1 - core)
+        leaf_ym[...] = jnp.broadcast_to(mask_lanes(k), leaf_ym.shape).astype(BF16)
+        value = answer.at[k]
 
         def tile(i, _):
             columns = pl.ds(pl.multiple_of(i * TILE, TILE), TILE)
-            term = dot_cols(answer_whole(k), couple[k, :, columns]) * leaf_ym[
-                :, columns
-            ].astype(F32)
-            back[:, columns] = term if k == 2 else back[:, columns] + term
+            term = dot_cols(
+                value[...].reshape(right_sides, size), couple[k, :, columns]
+            ) * leaf_ym[:, columns].astype(F32)
+            back[:, columns] = back[:, columns] - term
+            return 0
+
+        lax.fori_loop(0, size // TILE, tile, 0)
+
+    def leaf_end(side):
+        rows = pl.ds(pl.multiple_of(side * side_cols, side_cols), side_cols)
+
+        def tile(i, _):
+            start = pl.multiple_of(i * TILE, TILE)
+            columns = pl.ds(start, TILE)
+            term = dot_cols(answer[0, side].reshape(side_cols, size), couple[0, :, columns])
+            target = (back[rows, columns] - term * leaf_ym[0:1, columns].astype(F32)).astype(BF16)
+            for j in range(TILE // blk):
+                b = i * (TILE // blk) + j
+                solved = dot_rows(lower_t[b], target[:, j * blk : (j + 1) * blk])
+                leaf_out[b, :, rows] = solved.astype(BF16)
             return 0
 
         lax.fori_loop(0, size // TILE, tile, 0)
@@ -619,21 +641,20 @@
         arrived(own_answer(0), x_recv.at[0])
         answer_first(0, is_odd)
 
+    diag_lanes = jnp.concatenate([diag[b : b + 1, :] for b in range(blocks)], axis=1)
+    back[...] = leaf_y[...].astype(F32) / diag_lanes
     leaf_back(2)
     answer_second(1)
     answer_second(0)
     answer_third(1)
     leaf_back(1)
     answer_third(0)
-    leaf_back(0)
-
-    def solve_back(b, _):
-        columns = pl.ds(pl.multiple_of(b * blk, blk), blk)
-        target = leaf_y[:, columns].astype(F32) / diag[pl.ds(b, 1), :] - back[:, columns]
-        leaf_out[b] = dot_rows(lower_t[b], target.astype(BF16)).astype(BF16)
-        return 0
-
-    lax.fori_loop(0, blocks, solve_back, 0)
+    leaf_ym[0:16, :] = jnp.broadcast_to(mask_lanes(0), (16, size)).astype(BF16)
+    rows_out(0, core)
+    leaf_end(core)
+    answer_end(0)
+    leaf_end(1 - core)
+    rows_out(0, 1 - core)
 
     for when, make in sends:
         if when is None:
@@ -664,6 +685,7 @@
     cols = right_sides // (SIDE * SIDE * CORES)
     half = size // 2
     grid = (SIDE, SIDE, CORES)
+    sides = (CORES, SIDE, SIDE)
     vmem = pltpu.VMEM
     dma = pltpu.SemaphoreType.DMA
     hops = (levels, 2, 2, SIDE - 1)
@@ -681,7 +703,7 @@
         vmem((right_sides, blocks * blk), BF16),
         vmem((right_sides, blocks * blk), BF16),
         vmem(leaf_inverse.shape, BF16),
-        vmem((levels,) + grid + (cols, size), BF16),
+        vmem((levels,) + sides + (cols, size), BF16),
         vmem((levels, SIDE, SIDE, cols, size), BF16),
         vmem((levels, SIDE, SIDE, cols, size), BF16),
         vmem((levels, 2, SIDE - 1, SIDE, cols, half), BF16),
@@ -696,7 +718,7 @@
         vmem((2, cols, size), BF16),
         vmem((cols, size), BF16),
         vmem((cols, size), F32),
-        vmem((levels,) + grid + (cols, size), BF16),
+        vmem((levels,) + sides + (cols, size), BF16),
         vmem((right_sides, blocks * blk), F32),
         dma((10,)),
         dma((levels, blocks)),
@@ -736,7 +758,7 @@
             collective_id=0, has_side_effects=True, vmem_limit_bytes=56 * 2**20
         ),
     )(
-        couple_mask,
+        couple_mask.T,
         leaf_rhs,
         leaf_inverse,
         leaf_couple,

time: 102 us -> 104 us (1.020)
  Pallas kernels: 95.8 us -> 99.4 us
  local copies, waits for them, and re-layouts: 5.15 us -> 3.8 us
    pallas_call x1, Pallas kernels: 95.8 us -> 99.4 us  [body(): pl.pallas_call(kernel, out_shape=(jax.ShapeDtypeStruct(leaf_rhs.shape, BF...]
    unnamed x3 -> x2, local copies, waits for them, and re-layouts: 5.15 us -> 3.8 us
where the time goes in v2:
time: 104 us
  Pallas kernels  99.4 us (96%)
  local copies, waits for them, and re-layouts  3.8 us (4%)
    pallas_call x1, Pallas kernels, body(): pl.pallas_call(kernel, out_shape=(jax.ShapeDtypeStruct(leaf_rhs.shape, BF...  99.4 us
    unnamed x2, local copies, waits for them, and re-layouts  3.8 us

profile of v2, /device:TPU:1, one launch (start us, length us, event | category | flops | bytes accessed | tf_op | source)
XLA Modules:
  0.0 103.9 jit_solution(3977202646431838871)
XLA Ops:
  0.6 99.4 %shard_map.104 = (bf16[8,128,512]{2,1,0:T(8,128)(2,1)}, bf16[1,3,32,512]{3,2,1,0:T(8,128)(2,1)}) custom-call(s32[3,8]{1,0:T(4,128)} %bitcast.1, bf16[8,128,512]{2,1,0:T(8,128)(2,1)} %rhs_hbm.1, bf16[8,128,128]{2,1,0:T(8,128)(2,1)} %inverse_hbm.1, bf16[8,3,1024,128]{3,2,1,0:T(8,128)(2,1)} %couple_hbm.1, f32[8,128]{1,0:T(8,128)} %diag_hbm.1, ...), custom_call_target="tpu_custom_call" | custom-call | tf_op jit(solution)/shard_map/pallas_call | solution.py:748
  100.1 2.3 %copy.13 = bf16[8,128,512]{2,1,0:T(8,128)(2,1)} copy(bf16[8,128,512]{2,1,0:T(8,128)(2,1)} %get-tuple-element.4) | data formatting | bytes 2097152
  102.3 1.5 %copy.14 = bf16[1,3,32,512]{3,2,1,0:T(8,128)(2,1)} copy(bf16[1,3,32,512]{3,2,1,0:T(8,128)(2,1)} %get-tuple-element.5) | data formatting | bytes 196608

commit v3 on v2

--- a/solution.py
+++ b/solution.py
@@ -63,11 +63,16 @@
     total,
     from_odd,
     out_total,
+    from_all,
     to_two,
     from_one,
     to_three,
     from_two,
     sep_y,
+    helped_y,
+    helped,
+    carry,
+    carried,
     sep_z,
     answer,
     back,
@@ -91,6 +96,12 @@
     two_recv,
     three_send,
     three_recv,
+    all_send,
+    all_recv,
+    y_send,
+    y_recv,
+    carry_send,
+    carry_recv,
     x_send,
     x_recv,
 ):
@@ -121,10 +132,16 @@
     is_odd = layer % 2 == 1
     is_two = layer % 4 == 1
     is_three = layer == 3
+    not_three = layer != 3
+    is_helper = layer % 4 == 3
+    is_seven = layer == 7
     has_first = layer != 7
-    has_second = jnp.logical_or(is_one, is_two)
     sep_of = [layer // 2, 4 + layer // 4, 6 + layer * 0]
     own_sep = jnp.where(is_one, layer // 2, jnp.where(is_two, 4 + layer // 4, 6))
+
+    second_sep = jnp.where(is_helper, layer // 2, own_sep)
+    second_block = jnp.where(is_helper, 1, 0)
+    third_sep = ((layer + 1) % 8) // 2
 
     sends = []
 
@@ -143,6 +160,12 @@
         make().start()
         sends.append((when, make))
 
+    def only(when, act):
+        if when is None:
+            act()
+        else:
+            pl.when(when)(act)
+
     def arrived(dst, sem):
         pltpu.make_async_copy(dst, dst, sem).wait()
 
@@ -158,8 +181,12 @@
     local = [
         pltpu.make_async_copy(sep_inverse_hbm.at[own_sep], own_inverse, local_sem.at[0]),
         pltpu.make_async_copy(sep_diag_hbm, own_diag, local_sem.at[1]),
-        pltpu.make_async_copy(sep_couple_hbm.at[own_sep, 0], mat1.at[y, x, core], local_sem.at[2]),
-        pltpu.make_async_copy(sep_couple_hbm.at[own_sep, 1], mat2.at[y, x, core], local_sem.at[3]),
+        pltpu.make_async_copy(
+            sep_couple_hbm.at[second_sep, second_block], mat1.at[y, x, core], local_sem.at[2]
+        ),
+        pltpu.make_async_copy(
+            sep_couple_hbm.at[third_sep, 1], mat2.at[y, x, core], local_sem.at[3]
+        ),
         pltpu.make_async_copy(inverse_hbm, inverse, local_sem.at[4]),
         pltpu.make_async_copy(rhs_hbm, rhs, local_sem.at[5]),
         pltpu.make_async_copy(diag_hbm, diag, local_sem.at[6]),
@@ -242,7 +269,7 @@
         arrived(pick(everywhere, everywhere, 1 - core, everywhere), c_recv)
 
     mats = [mat0, mat1, mat2]
-    uses = [has_first, has_second, is_one]
+    uses = [has_first, None, is_helper]
 
     def whole(m):
         return mats[m][:, :, :, :, 0:size].reshape(size, size)
@@ -256,19 +283,13 @@
         )
 
     def mat_first(m):
-        @pl.when(uses[m])
-        def _():
-            gather_first(*mat_parts(m)[:3], uses[m])
+        only(uses[m], lambda: gather_first(*mat_parts(m)[:3], uses[m]))
 
     def mat_second(m):
-        @pl.when(uses[m])
-        def _():
-            gather_second(*mat_parts(m)[:3], uses[m])
+        only(uses[m], lambda: gather_second(*mat_parts(m)[:3], uses[m]))
 
     def mat_third(m):
-        @pl.when(uses[m])
-        def _():
-            gather_third(*mat_parts(m), uses[m])
+        only(uses[m], lambda: gather_third(*mat_parts(m), uses[m]))
 
     def mat_end(m):
         gather_end(mat_parts(m)[0], gc_recv.at[m])
@@ -404,19 +425,35 @@
                 value = value + in2[k, h, d - 1].astype(F32)
             total[k, :, h * half : (h + 1) * half] = value
 
-        @pl.when(is_odd)
-        def _():
+        def send():
             out_total[k] = total[k].astype(BF16)
-            remote(
-                lambda: (
-                    out_total.at[k],
-                    from_odd.at[k],
-                    odd_send.at[k],
-                    odd_recv.at[k],
-                    ((layer + 7) % 8, plane),
-                ),
-                is_odd,
-            )
+            if k < 2:
+                remote(
+                    lambda: (
+                        out_total.at[k],
+                        from_odd.at[k],
+                        odd_send.at[k],
+                        odd_recv.at[k],
+                        ((layer + 7) % 8, plane),
+                    ),
+                    is_odd,
+                )
+            else:
+                remote(
+                    lambda: (
+                        out_total.at[k],
+                        from_all.at[slot_of_all()],
+                        all_send,
+                        all_recv.at[slot_of_all()],
+                        (3, plane),
+                    ),
+                    not_three,
+                )
+
+        pl.when(is_odd if k < 2 else not_three)(send)
+
+    def slot_of_all():
+        return layer - jnp.where(layer > 3, 1, 0)
 
     def whole_total(k):
         arrived(from_odd.at[k], odd_recv.at[k])
@@ -455,61 +492,74 @@
         residual = whole_total(0)
         mat_end(0)
         forward(residual)
+        remote(
+            lambda: (
+                sep_y,
+                helped_y.at[1 - two_slot],
+                y_send,
+                y_recv.at[1 - two_slot],
+                ((layer + 7 + 2 * two_slot) % 8, plane),
+            ),
+            is_one,
+        )
 
     reduce_first(2)
     reduce_end(1)
     mat_third(1)
-    reduce_second(2)
-
-    def pass_up(k):
-        to_two[k - 1] = (whole_total(k) - dot_rows(sep_y[...], whole(k))).astype(BF16)
+
+    @pl.when(is_one)
+    def _():
+        mat_end(1)
+        to_two[...] = (whole_total(1) - dot_rows(sep_y[...], whole(1))).astype(BF16)
         remote(
             lambda: (
-                to_two.at[k - 1],
-                from_one.at[two_slot, k - 1],
-                two_send.at[k - 1],
-                two_recv.at[two_slot, k - 1],
+                to_two,
+                from_one.at[two_slot],
+                two_send,
+                two_recv.at[two_slot],
                 (two_of, plane),
             ),
             is_one,
         )
 
-    @pl.when(is_one)
+    reduce_second(2)
+    mat_third(2)
+    reduce_end(2)
+
+    @pl.when(is_helper)
     def _():
         mat_end(1)
-        pass_up(1)
-
-    reduce_end(2)
-    mat_third(2)
-
-    @pl.when(is_one)
-    def _():
         mat_end(2)
-        pass_up(2)
+        for slot in range(2):
+            arrived(helped_y.at[slot], y_recv.at[slot])
+        helped[...] = dot_rows(helped_y[0], whole(1)) + dot_rows(helped_y[1], whole(2))
+
+    def send_three(slot, when):
+        remote(
+            lambda: (
+                to_three,
+                from_two.at[slot()],
+                three_send,
+                three_recv.at[slot()],
+                (3, plane),
+            ),
+            when,
+        )
+
+    @pl.when(is_seven)
+    def _():
+        to_three[...] = helped[...].astype(BF16)
+        send_three(lambda: 2, is_seven)
 
     @pl.when(is_two)
     def _():
         mat_end(0)
         mat_end(1)
         for slot in range(2):
-            arrived(from_one.at[slot, 0], two_recv.at[slot, 0])
-        forward(from_one[0, 0].astype(F32) + from_one[1, 0].astype(F32))
-        term = dot_rows(sep_y[...], whole(1))
-        for slot in range(2):
-            arrived(from_one.at[slot, 1], two_recv.at[slot, 1])
-        to_three[...] = (from_one[0, 1].astype(F32) + from_one[1, 1].astype(F32) - term).astype(
-            BF16
-        )
-        remote(
-            lambda: (
-                to_three,
-                from_two.at[layer // 4],
-                three_send,
-                three_recv.at[layer // 4],
-                (3, plane),
-            ),
-            is_two,
-        )
+            arrived(from_one.at[slot], two_recv.at[slot])
+        forward(from_one[0].astype(F32) + from_one[1].astype(F32))
+        to_three[...] = dot_rows(sep_y[...], whole(1)).astype(BF16)
+        send_three(lambda: layer // 4, is_two)
 
     def finish(k, target):
         answer[k, core, y, x] = dot_cols(target.astype(BF16), whole(0)).astype(BF16)
@@ -532,12 +582,29 @@
     @pl.when(is_three)
     def _():
         mat_end(0)
-        for slot in range(2):
+        residual = total[2] - helped[...]
+        for slot in range(7):
+            arrived(from_all.at[slot], all_recv.at[slot])
+            residual = residual + from_all[slot].astype(F32)
+        for slot in (2, 0, 1):
             arrived(from_two.at[slot], three_recv.at[slot])
-        forward(from_two[0].astype(F32) + from_two[1].astype(F32))
+            residual = residual - from_two[slot].astype(F32)
+        forward(residual)
         finish(2, sep_z[...])
-        for slot, layer_to in enumerate((1, 5, 2, 4, 0, 6, 7)):
+        for slot, layer_to in enumerate((1, 5, 7, 2, 4, 0, 6)):
             send_answer(2, slot, lambda layer_to=layer_to: layer_to, is_three)
+
+    def send_carry(slot):
+        remote(
+            lambda: (
+                carry.at[slot],
+                carried,
+                carry_send.at[slot],
+                carry_recv,
+                ((layer + 7 + 2 * slot) % 8, plane),
+            ),
+            is_helper,
+        )
 
     @pl.when(jnp.logical_not(is_three))
     def _():
@@ -569,21 +636,25 @@
     def answer_end(k):
         gather_end(answer_parts(k)[0], ac_recv.at[k])
 
+    @pl.when(is_helper)
+    def _():
+        for slot in range(2):
+            term = dot_cols(own_answer(2)[...], whole(1 + slot))
+            carry[slot] = term.astype(BF16)
+            send_carry(slot)
+
     answer_first(2)
+    answer_second(2)
+
+    @pl.when(jnp.logical_not(is_two))
+    def _():
+        arrived(own_answer(1), x_recv.at[1])
 
     @pl.when(is_one)
     def _():
-        sep_z[...] = sep_z[...] - dot_cols(own_answer(2)[...], whole(2))
-
-    answer_second(2)
-
-    @pl.when(jnp.logical_not(is_two))
-    def _():
-        arrived(own_answer(1), x_recv.at[1])
-
-    @pl.when(is_one)
-    def _():
-        finish(0, sep_z[...] - dot_cols(own_answer(1)[...], whole(1)))
+        term = dot_cols(own_answer(1)[...], whole(1))
+        arrived(carried, carry_recv)
+        finish(0, sep_z[...] - carried[...].astype(F32) - term)
         send_answer(0, 10, lambda: layer + 1, is_one)
         answer_first(0, is_one)
 
@@ -659,13 +730,25 @@
     for when, make in sends:
         if when is None:
             make().wait_send()
-    for group in (has_first, has_second, is_one, is_odd, is_two, is_three):
+    for group in (has_first, is_helper, is_one, is_odd, is_two, is_three, not_three, is_seven):
 
         @pl.when(group)
         def _(group=group):
             for when, make in sends:
                 if when is group:
                     make().wait_send()
+
+
+def copy_kernel(leaf_ref, sep_ref, leaf_out, sep_out, sems):
+    blocks = leaf_ref.shape[0]
+    copies = [
+        pltpu.make_async_copy(leaf_ref.at[b], leaf_out.at[b], sems.at[b]) for b in range(blocks)
+    ]
+    copies.append(pltpu.make_async_copy(sep_ref, sep_out, sems.at[blocks]))
+    for copy in copies:
+        copy.start()
+    for copy in copies:
+        copy.wait()
 
 
 def body(
@@ -712,9 +795,14 @@
         vmem((levels, cols, size), F32),
         vmem((levels, cols, size), BF16),
         vmem((levels, cols, size), BF16),
+        vmem((7, cols, size), BF16),
+        vmem((cols, size), BF16),
         vmem((2, cols, size), BF16),
-        vmem((2, 2, cols, size), BF16),
         vmem((cols, size), BF16),
+        vmem((3, cols, size), BF16),
+        vmem((cols, size), BF16),
+        vmem((2, cols, size), BF16),
+        vmem((cols, size), F32),
         vmem((2, cols, size), BF16),
         vmem((cols, size), BF16),
         vmem((cols, size), F32),
@@ -734,18 +822,24 @@
         dma(hops),
         dma((levels,)),
         dma((levels,)),
-        dma((levels,)),
-        dma((levels,)),
         dma((2,)),
-        dma((2, 2)),
+        dma((2,)),
         dma,
         dma((2,)),
+        dma,
+        dma((3,)),
+        dma,
+        dma((7,)),
+        dma,
+        dma((2,)),
+        dma((2,)),
+        dma,
         dma((11,)),
         dma((levels,)),
     ]
     any_space = pl.BlockSpec(memory_space=pl.ANY)
     in_vmem = pl.BlockSpec(memory_space=pltpu.VMEM)
-    return pl.pallas_call(
+    outs = pl.pallas_call(
         kernel,
         out_shape=(
             jax.ShapeDtypeStruct(leaf_rhs.shape, BF16),
@@ -768,6 +862,13 @@
         sep_couple,
         sep_diag,
     )
+    return pl.pallas_call(
+        copy_kernel,
+        out_shape=tuple(jax.ShapeDtypeStruct(out.shape, out.dtype) for out in outs),
+        in_specs=[any_space] * 2,
+        out_specs=(any_space, any_space),
+        scratch_shapes=[dma((blocks + 1,))],
+    )(*outs)
 
 
 def solution(mesh):

time: 104 us -> 129 us (1.24)
  Pallas kernels: 99.4 us -> 128 us
  local copies, waits for them, and re-layouts: 3.8 us -> 0 us
    pallas_call x0 -> x1, Pallas kernels: none -> 35.9 us  [body(): pl.pallas_call(copy_kernel, out_shape=tuple((jax.ShapeDtypeStruct(out.sha...]
    pallas_call x1, Pallas kernels: 99.4 us -> 92 us  [body(): pl.pallas_call(kernel, out_shape=(jax.ShapeDtypeStruct(leaf_rhs.shape, BF...]
    unnamed x2 -> x0, local copies, waits for them, and re-layouts: 3.8 us -> none
where the time goes in v3:
time: 129 us
  Pallas kernels  128 us (99%)
    pallas_call x1, Pallas kernels, body(): pl.pallas_call(kernel, out_shape=(jax.ShapeDtypeStruct(leaf_rhs.shape, BF...  92 us
    pallas_call x1, Pallas kernels, body(): pl.pallas_call(copy_kernel, out_shape=tuple((jax.ShapeDtypeStruct(out.sha...  35.9 us

profile of v3, /device:TPU:1, one launch (start us, length us, event | category | flops | bytes accessed | tf_op | source)
XLA Modules:
  0.0 128.5 jit_solution(3529725918639570905)
XLA Ops:
  0.6 92.0 %shard_map.104 = (bf16[8,128,512]{2,1,0:T(8,128)(2,1)}, bf16[1,3,32,512]{3,2,1,0:T(8,128)(2,1)}) custom-call(s32[3,8]{1,0:T(4,128)} %bitcast.1, bf16[8,128,512]{2,1,0:T(8,128)(2,1)} %rhs_hbm.1, bf16[8,128,128]{2,1,0:T(8,128)(2,1)} %inverse_hbm.1, bf16[8,3,1024,128]{3,2,1,0:T(8,128)(2,1)} %couple_hbm.1, f32[8,128]{1,0:T(8,128)} %diag_hbm.1, ...), custom_call_target="tpu_custom_call" | custom-call | tf_op jit(solution)/shard_map/pallas_call | solution.py:842
  92.6 35.9 %shard_map.105 = (bf16[8,128,512]{2,1,0:T(8,128)(2,1)}, bf16[1,3,32,512]{3,2,1,0:T(8,128)(2,1)}) custom-call(bf16[8,128,512]{2,1,0:T(8,128)(2,1)} %get-tuple-element.4.leaf_ref, bf16[1,3,32,512]{3,2,1,0:T(8,128)(2,1)} %get-tuple-element.5.sep_ref), custom_call_target="tpu_custom_call" | custom-call | tf_op jit(solution)/shard_map/pallas_call | solution.py:865

commit v4 on v3

--- a/solution.py
+++ b/solution.py
@@ -479,11 +479,11 @@
     reduce_first(0)
     mat_second(0)
     leaf_part(2)
+    reduce_second(0)
     reduce_first(1)
     mat_second(1)
-    reduce_second(0)
+    reduce_end(0)
     mat_third(0)
-    reduce_end(0)
     reduce_second(1)
     mat_second(2)
 
@@ -739,16 +739,9 @@
                     make().wait_send()
 
 
-def copy_kernel(leaf_ref, sep_ref, leaf_out, sep_out, sems):
-    blocks = leaf_ref.shape[0]
-    copies = [
-        pltpu.make_async_copy(leaf_ref.at[b], leaf_out.at[b], sems.at[b]) for b in range(blocks)
-    ]
-    copies.append(pltpu.make_async_copy(sep_ref, sep_out, sems.at[blocks]))
-    for copy in copies:
-        copy.start()
-    for copy in copies:
-        copy.wait()
+def copy_kernel(leaf_ref, sep_ref, leaf_out, sep_out):
+    leaf_out[...] = leaf_ref[...]
+    sep_out[...] = sep_ref[...]
 
 
 def body(
@@ -865,9 +858,8 @@
     return pl.pallas_call(
         copy_kernel,
         out_shape=tuple(jax.ShapeDtypeStruct(out.shape, out.dtype) for out in outs),
-        in_specs=[any_space] * 2,
-        out_specs=(any_space, any_space),
-        scratch_shapes=[dma((blocks + 1,))],
+        in_specs=[in_vmem] * 2,
+        out_specs=(in_vmem, in_vmem),
     )(*outs)
 
 

time: 129 us -> 93.2 us (0.72)
  Pallas kernels: 128 us -> 92.4 us
    pallas_call x1, Pallas kernels: 35.9 us -> 2.28 us  [body(): pl.pallas_call(copy_kernel, out_shape=tuple((jax.ShapeDtypeStruct(out.sha...]
    pallas_call x1, Pallas kernels: 92 us -> 90.1 us  [body(): pl.pallas_call(kernel, out_shape=(jax.ShapeDtypeStruct(leaf_rhs.shape, BF...]
where the time goes in v4:
time: 93.2 us; the launch traced here: 93 us
  Pallas kernels  92.4 us (99%)
    pallas_call x1, Pallas kernels, body(): pl.pallas_call(kernel, out_shape=(jax.ShapeDtypeStruct(leaf_rhs.shape, BF...  90.1 us
    pallas_call x1, Pallas kernels, body(): pl.pallas_call(copy_kernel, out_shape=tuple((jax.ShapeDtypeStruct(out.sha...  2.28 us

profile of v4, /device:TPU:1, one launch (start us, length us, event | category | flops | bytes accessed | tf_op | source)
XLA Modules:
  0.0 93.0 jit_solution(18059077536995155015)
XLA Ops:
  0.6 90.1 %shard_map.104 = (bf16[8,128,512]{2,1,0:T(8,128)(2,1)}, bf16[1,3,32,512]{3,2,1,0:T(8,128)(2,1)}) custom-call(s32[3,8]{1,0:T(4,128)} %bitcast.1, bf16[8,128,512]{2,1,0:T(8,128)(2,1)} %rhs_hbm.1, bf16[8,128,128]{2,1,0:T(8,128)(2,1)} %inverse_hbm.1, bf16[8,3,1024,128]{3,2,1,0:T(8,128)(2,1)} %couple_hbm.1, f32[8,128]{1,0:T(8,128)} %diag_hbm.1, ...), custom_call_target="tpu_custom_call" | custom-call | tf_op jit(solution)/shard_map/pallas_call | solution.py:835
  90.7 2.3 %shard_map.105 = (bf16[8,128,512]{2,1,0:T(8,128)(2,1)}, bf16[1,3,32,512]{3,2,1,0:T(8,128)(2,1)}) custom-call(bf16[8,128,512]{2,1,0:T(8,128)(2,1)} %get-tuple-element.4.leaf_ref, bf16[1,3,32,512]{3,2,1,0:T(8,128)(2,1)} %get-tuple-element.5.sep_ref), custom_call_target="tpu_custom_call" | custom-call | tf_op jit(solution)/shard_map/pallas_call | solution.py:858

commit v5 on v4

--- a/solution.py
+++ b/solution.py
@@ -479,8 +479,8 @@
     reduce_first(0)
     mat_second(0)
     leaf_part(2)
+    reduce_first(1)
     reduce_second(0)
-    reduce_first(1)
     mat_second(1)
     reduce_end(0)
     mat_third(0)
@@ -561,6 +561,9 @@
         to_three[...] = dot_rows(sep_y[...], whole(1)).astype(BF16)
         send_three(lambda: layer // 4, is_two)
 
+    diag_lanes = jnp.concatenate([diag[b : b + 1, :] for b in range(blocks)], axis=1)
+    back[...] = leaf_y[...].astype(F32) / diag_lanes
+
     def finish(k, target):
         answer[k, core, y, x] = dot_cols(target.astype(BF16), whole(0)).astype(BF16)
 
@@ -705,18 +708,16 @@
         lax.fori_loop(0, size // TILE, tile, 0)
 
     answer_first(1)
-    answer_third(2)
+    answer_second(1)
 
     @pl.when(is_odd)
     def _():
         arrived(own_answer(0), x_recv.at[0])
         answer_first(0, is_odd)
 
-    diag_lanes = jnp.concatenate([diag[b : b + 1, :] for b in range(blocks)], axis=1)
-    back[...] = leaf_y[...].astype(F32) / diag_lanes
+    answer_third(2)
+    answer_second(0)
     leaf_back(2)
-    answer_second(1)
-    answer_second(0)
     answer_third(1)
     leaf_back(1)
     answer_third(0)

time: 93.2 us -> 91.2 us (0.979)
  Pallas kernels: 92.4 us -> 90.2 us
    pallas_call x1, Pallas kernels: 90.1 us -> 87.9 us  [body(): pl.pallas_call(kernel, out_shape=(jax.ShapeDtypeStruct(leaf_rhs.shape, BF...]
where the time goes in v5:
time: 91.2 us; the launch traced here: 90.8 us
  Pallas kernels  90.2 us (99%)
    pallas_call x1, Pallas kernels, body(): pl.pallas_call(kernel, out_shape=(jax.ShapeDtypeStruct(leaf_rhs.shape, BF...  87.9 us
    pallas_call x1, Pallas kernels, body(): pl.pallas_call(copy_kernel, out_shape=tuple((jax.ShapeDtypeStruct(out.sha...  2.28 us

profile of v5, /device:TPU:1, one launch (start us, length us, event | category | flops | bytes accessed | tf_op | source)
XLA Modules:
  0.0 90.8 jit_solution(15655656964993722022)
XLA Ops:
  0.6 87.9 %shard_map.104 = (bf16[8,128,512]{2,1,0:T(8,128)(2,1)}, bf16[1,3,32,512]{3,2,1,0:T(8,128)(2,1)}) custom-call(s32[3,8]{1,0:T(4,128)} %bitcast.1, bf16[8,128,512]{2,1,0:T(8,128)(2,1)} %rhs_hbm.1, bf16[8,128,128]{2,1,0:T(8,128)(2,1)} %inverse_hbm.1, bf16[8,3,1024,128]{3,2,1,0:T(8,128)(2,1)} %couple_hbm.1, f32[8,128]{1,0:T(8,128)} %diag_hbm.1, ...), custom_call_target="tpu_custom_call" | custom-call | tf_op jit(solution)/shard_map/pallas_call | solution.py:836
  88.5 2.3 %shard_map.105 = (bf16[8,128,512]{2,1,0:T(8,128)(2,1)}, bf16[1,3,32,512]{3,2,1,0:T(8,128)(2,1)}) custom-call(bf16[8,128,512]{2,1,0:T(8,128)(2,1)} %get-tuple-element.4.leaf_ref, bf16[1,3,32,512]{3,2,1,0:T(8,128)(2,1)} %get-tuple-element.5.sep_ref), custom_call_target="tpu_custom_call" | custom-call | tf_op jit(solution)/shard_map/pallas_call | solution.py:859

commit v6 on v5

--- a/solution.py
+++ b/solution.py
@@ -51,6 +51,9 @@
     mat0,
     mat1,
     mat2,
+    mat3,
+    mat4,
+    pair_inverse,
     leaf_y,
     leaf_ym,
     lower_t,
@@ -74,6 +77,7 @@
     carry,
     carried,
     sep_z,
+    pair_z,
     answer,
     back,
     local_sem,
@@ -99,6 +103,7 @@
     all_send,
     all_recv,
     y_send,
+    y_pair_send,
     y_recv,
     carry_send,
     carry_recv,
@@ -135,6 +140,7 @@
     not_three = layer != 3
     is_helper = layer % 4 == 3
     is_seven = layer == 7
+    is_base = layer % 4 == 0
     has_first = layer != 7
     sep_of = [layer // 2, 4 + layer // 4, 6 + layer * 0]
     own_sep = jnp.where(is_one, layer // 2, jnp.where(is_two, 4 + layer // 4, 6))
@@ -193,6 +199,10 @@
         pltpu.make_async_copy(sep_rhs_hbm.at[sep_of[0]], sep_rhs.at[0], local_sem.at[7]),
         pltpu.make_async_copy(sep_rhs_hbm.at[sep_of[1]], sep_rhs.at[1], local_sem.at[8]),
         pltpu.make_async_copy(sep_rhs_hbm.at[sep_of[2]], sep_rhs.at[2], local_sem.at[9]),
+        pltpu.make_async_copy(sep_inverse_hbm.at[sep_of[0]], pair_inverse, local_sem.at[10]),
+        pltpu.make_async_copy(
+            sep_couple_hbm.at[sep_of[0], 0], mat4.at[y, x, core], local_sem.at[11]
+        ),
     ]
     for copy in local:
         copy.start()
@@ -268,8 +278,8 @@
         everywhere = slice(None)
         arrived(pick(everywhere, everywhere, 1 - core, everywhere), c_recv)
 
-    mats = [mat0, mat1, mat2]
-    uses = [has_first, None, is_helper]
+    mats = [mat0, mat1, mat2, mat3, mat4]
+    uses = [has_first, None, is_helper, is_odd, is_odd]
 
     def whole(m):
         return mats[m][:, :, :, :, 0:size].reshape(size, size)
@@ -299,19 +309,22 @@
     eye = lax.broadcasted_iota(jnp.int32, (own_rows, own_rows), 0) == lax.broadcasted_iota(
         jnp.int32, (own_rows, own_rows), 1
     )
-    sep_rows = lax.broadcasted_iota(jnp.int32, own_diag.shape, 0) == own_sep
-    diag_row = jnp.sum(jnp.where(sep_rows, own_diag[...], 0.0), axis=0, keepdims=True)
-    diag_col = jnp.sum(jnp.where(eye, diag_row, 0.0), axis=1, keepdims=True)
-    high = diag_col.astype(BF16).astype(F32)
-    middle = (diag_col - high).astype(BF16).astype(F32)
-    low = diag_col - high - middle
-    lane = lax.broadcasted_iota(jnp.int32, (own_rows, EXTRA), 1)
-    beside = jnp.where(
-        lane == 0, high, jnp.where(lane == 1, middle, jnp.where(lane == 2, low, 0.0))
-    ).astype(BF16)
+
+    def diag_beside(sep):
+        sep_rows = lax.broadcasted_iota(jnp.int32, own_diag.shape, 0) == sep
+        diag_row = jnp.sum(jnp.where(sep_rows, own_diag[...], 0.0), axis=0, keepdims=True)
+        diag_col = jnp.sum(jnp.where(eye, diag_row, 0.0), axis=1, keepdims=True)
+        high = diag_col.astype(BF16).astype(F32)
+        middle = (diag_col - high).astype(BF16).astype(F32)
+        low = diag_col - high - middle
+        lane = lax.broadcasted_iota(jnp.int32, (own_rows, EXTRA), 1)
+        return jnp.where(
+            lane == 0, high, jnp.where(lane == 1, middle, jnp.where(lane == 2, low, 0.0))
+        ).astype(BF16)
+
     mat0[y, x, core, :, 0:size] = unit_lower(own_inverse[...], first_row)
-    mat0[y, x, core, :, size:] = beside
-    for i in range(4, 10):
+    mat0[y, x, core, :, size:] = diag_beside(own_sep)
+    for i in range(4, 12):
         local[i].wait()
 
     def solve_leaf(b, _):
@@ -323,6 +336,8 @@
         return 0
 
     lax.fori_loop(0, blocks, solve_leaf, 0)
+    mat3[y, x, core, :, 0:size] = unit_lower(pair_inverse[...], first_row)
+    mat3[y, x, core, :, size:] = diag_beside(sep_of[0])
 
     pl.semaphore_wait(barrier, len(peers))
     mat_first(0)
@@ -459,11 +474,11 @@
         arrived(from_odd.at[k], odd_recv.at[k])
         return total[k] + from_odd[k].astype(F32)
 
-    def divide(value):
+    def divide(value, m=0):
         picks = jnp.where(
             lax.broadcasted_iota(jnp.int32, (value.shape[0], EXTRA), 1) < 3, 1.0, 0.0
         ).astype(BF16)
-        parts = mat0[:, :, :, :, size:].reshape(size, EXTRA)
+        parts = mats[m][:, :, :, :, size:].reshape(size, EXTRA)
         return value / dot_rows(picks, parts)
 
     def forward(residual):
@@ -503,9 +518,18 @@
             is_one,
         )
 
+    @pl.when(is_base)
+    def _():
+        remote(
+            lambda: (sep_y, helped_y.at[0], y_pair_send, y_recv.at[0], (layer + 1, plane)),
+            is_base,
+        )
+
     reduce_first(2)
     reduce_end(1)
     mat_third(1)
+    mat_first(3)
+    mat_first(4)
 
     @pl.when(is_one)
     def _():
@@ -525,6 +549,8 @@
     reduce_second(2)
     mat_third(2)
     reduce_end(2)
+    mat_second(3)
+    mat_second(4)
 
     @pl.when(is_helper)
     def _():
@@ -564,8 +590,8 @@
     diag_lanes = jnp.concatenate([diag[b : b + 1, :] for b in range(blocks)], axis=1)
     back[...] = leaf_y[...].astype(F32) / diag_lanes
 
-    def finish(k, target):
-        answer[k, core, y, x] = dot_cols(target.astype(BF16), whole(0)).astype(BF16)
+    def finish(k, target, m=0):
+        answer[k, core, y, x] = dot_cols(target.astype(BF16), whole(m)).astype(BF16)
 
     def own_answer(k):
         return answer.at[k, core, y, x]
@@ -597,17 +623,33 @@
         for slot, layer_to in enumerate((1, 5, 7, 2, 4, 0, 6)):
             send_answer(2, slot, lambda layer_to=layer_to: layer_to, is_three)
 
-    def send_carry(slot):
+    def send_carry(slot, to):
         remote(
             lambda: (
                 carry.at[slot],
                 carried,
-                carry_send.at[slot],
+                carry_send.at[to],
                 carry_recv,
-                ((layer + 7 + 2 * slot) % 8, plane),
+                ((layer + (7, 1, 2)[to]) % 8, plane),
             ),
             is_helper,
         )
+
+    mat_third(3)
+    mat_third(4)
+
+    @pl.when(is_odd)
+    def _():
+        mat_end(3)
+
+    @pl.when(is_two)
+    def _():
+        arrived(helped_y.at[0], y_recv.at[0])
+
+    @pl.when(is_odd)
+    def _():
+        pair_z[...] = divide(helped_y[0].astype(F32), 3)
+        mat_end(4)
 
     @pl.when(jnp.logical_not(is_three))
     def _():
@@ -627,8 +669,8 @@
             lambda: (ac_send.at[k], ac_recv.at[k]),
         )
 
-    def answer_first(k, when=None):
-        gather_first(*answer_parts(k)[:3], when)
+    def answer_first(k):
+        gather_first(*answer_parts(k)[:3])
 
     def answer_second(k):
         gather_second(*answer_parts(k)[:3])
@@ -644,7 +686,8 @@
         for slot in range(2):
             term = dot_cols(own_answer(2)[...], whole(1 + slot))
             carry[slot] = term.astype(BF16)
-            send_carry(slot)
+            send_carry(slot, slot)
+        send_carry(1, 2)
 
     answer_first(2)
     answer_second(2)
@@ -653,13 +696,25 @@
     def _():
         arrived(own_answer(1), x_recv.at[1])
 
+    @pl.when(jnp.logical_not(is_helper))
+    def _():
+        arrived(carried, carry_recv)
+
+    @pl.when(is_helper)
+    def _():
+        carried[...] = carry[0]
+
     @pl.when(is_one)
     def _():
         term = dot_cols(own_answer(1)[...], whole(1))
-        arrived(carried, carry_recv)
         finish(0, sep_z[...] - carried[...].astype(F32) - term)
-        send_answer(0, 10, lambda: layer + 1, is_one)
-        answer_first(0, is_one)
+
+    @pl.when(is_odd)
+    def _():
+        term = dot_cols(own_answer(1)[...], whole(4))
+        finish(0, pair_z[...] - carried[...].astype(F32) - term, 3)
+
+    answer_first(0)
 
     own_rows_at = jnp.where(
         first_row + lax.broadcasted_iota(jnp.int32, (own_rows, size), 0)
@@ -709,12 +764,6 @@
 
     answer_first(1)
     answer_second(1)
-
-    @pl.when(is_odd)
-    def _():
-        arrived(own_answer(0), x_recv.at[0])
-        answer_first(0, is_odd)
-
     answer_third(2)
     answer_second(0)
     leaf_back(2)
@@ -731,7 +780,7 @@
     for when, make in sends:
         if when is None:
             make().wait_send()
-    for group in (has_first, is_helper, is_one, is_odd, is_two, is_three, not_three, is_seven):
+    for group in (has_first, is_helper, is_one, is_odd, is_two, is_three, not_three, is_seven, is_base):
 
         @pl.when(group)
         def _(group=group):
@@ -777,6 +826,9 @@
         vmem(grid + (own_rows, size + EXTRA), BF16),
         vmem(grid + (own_rows, size), BF16),
         vmem(grid + (own_rows, size), BF16),
+        vmem(grid + (own_rows, size + EXTRA), BF16),
+        vmem(grid + (own_rows, size), BF16),
+        vmem((own_rows, size), BF16),
         vmem((right_sides, blocks * blk), BF16),
         vmem((right_sides, blocks * blk), BF16),
         vmem(leaf_inverse.shape, BF16),
@@ -800,14 +852,15 @@
         vmem((2, cols, size), BF16),
         vmem((cols, size), BF16),
         vmem((cols, size), F32),
+        vmem((cols, size), F32),
         vmem((levels,) + sides + (cols, size), BF16),
         vmem((right_sides, blocks * blk), F32),
-        dma((10,)),
+        dma((12,)),
         dma((levels, blocks)),
-        dma(hops),
-        dma(hops),
-        dma((levels,)),
-        dma((levels,)),
+        dma((5,) + hops[1:]),
+        dma((5,) + hops[1:]),
+        dma((5,)),
+        dma((5,)),
         dma(hops),
         dma(hops),
         dma((levels,)),
@@ -825,8 +878,9 @@
         dma,
         dma((7,)),
         dma,
+        dma,
         dma((2,)),
-        dma((2,)),
+        dma((3,)),
         dma,
         dma((11,)),
         dma((levels,)),

time: 91.2 us -> 97.1 us (1.065)
  the two profiles are of different devices: /device:TPU:1 before, /device:TPU:97 now
where the time goes in v6:
time: 97.1 us; the launch traced here: 97 us
  Pallas kernels  96.3 us (99%)
    pallas_call x1, Pallas kernels, body(): pl.pallas_call(kernel, out_shape=(jax.ShapeDtypeStruct(leaf_rhs.shape, BF...  94 us
    pallas_call x1, Pallas kernels, body(): pl.pallas_call(copy_kernel, out_shape=tuple((jax.ShapeDtypeStruct(out.sha...  2.28 us

profile of v6, /device:TPU:97, one launch (start us, length us, event | category | flops | bytes accessed | tf_op | source)
XLA Modules:
  0.0 97.0 jit_solution(9118966068874060306)
XLA Ops:
  0.6 94.0 %shard_map.104 = (bf16[8,128,512]{2,1,0:T(8,128)(2,1)}, bf16[1,3,32,512]{3,2,1,0:T(8,128)(2,1)}) custom-call(s32[3,8]{1,0:T(4,128)} %bitcast.1, bf16[8,128,512]{2,1,0:T(8,128)(2,1)} %rhs_hbm.1, bf16[8,128,128]{2,1,0:T(8,128)(2,1)} %inverse_hbm.1, bf16[8,3,1024,128]{3,2,1,0:T(8,128)(2,1)} %couple_hbm.1, f32[8,128]{1,0:T(8,128)} %diag_hbm.1, ...), custom_call_target="tpu_custom_call" | custom-call | tf_op jit(solution)/shard_map/pallas_call | solution.py:890
  94.7 2.3 %shard_map.105 = (bf16[8,128,512]{2,1,0:T(8,128)(2,1)}, bf16[1,3,32,512]{3,2,1,0:T(8,128)(2,1)}) custom-call(bf16[8,128,512]{2,1,0:T(8,128)(2,1)} %get-tuple-element.4.leaf_ref, bf16[1,3,32,512]{3,2,1,0:T(8,128)(2,1)} %get-tuple-element.5.sep_ref), custom_call_target="tpu_custom_call" | custom-call | tf_op jit(solution)/shard_map/pallas_call | solution.py:913

commit v7 on v5

--- a/solution.py
+++ b/solution.py
@@ -485,6 +485,7 @@
     reduce_end(0)
     mat_third(0)
     reduce_second(1)
+    reduce_first(2)
     mat_second(2)
 
     @pl.when(is_one)
@@ -503,9 +504,9 @@
             is_one,
         )
 
-    reduce_first(2)
     reduce_end(1)
     mat_third(1)
+    reduce_second(2)
 
     @pl.when(is_one)
     def _():
@@ -522,9 +523,8 @@
             is_one,
         )
 
-    reduce_second(2)
+    reduce_end(2)
     mat_third(2)
-    reduce_end(2)
 
     @pl.when(is_helper)
     def _():
@@ -833,6 +833,8 @@
     ]
     any_space = pl.BlockSpec(memory_space=pl.ANY)
     in_vmem = pl.BlockSpec(memory_space=pltpu.VMEM)
+    leaf_block = pl.BlockSpec((blocks // 4,) + leaf_rhs.shape[1:], lambda i: (i, 0, 0))
+    sep_block = pl.BlockSpec((1, levels, own_rows, right_sides), lambda i: (0, 0, 0, 0))
     outs = pl.pallas_call(
         kernel,
         out_shape=(
@@ -859,8 +861,9 @@
     return pl.pallas_call(
         copy_kernel,
         out_shape=tuple(jax.ShapeDtypeStruct(out.shape, out.dtype) for out in outs),
-        in_specs=[in_vmem] * 2,
-        out_specs=(in_vmem, in_vmem),
+        grid=(4,),
+        in_specs=[leaf_block, sep_block],
+        out_specs=(leaf_block, sep_block),
     )(*outs)
 
 

time: 91.2 us -> 92.4 us (1.013)
  Pallas kernels: 90.2 us -> 91.3 us
    pallas_call x1, Pallas kernels: 2.28 us -> 3.42 us  [body(): pl.pallas_call(copy_kernel, out_shape=tuple((jax.ShapeDtypeStruct(out.sha...]
where the time goes in v7:
time: 92.4 us; the launch traced here: 92 us
  Pallas kernels  91.3 us (99%)
    pallas_call x1, Pallas kernels, body(): pl.pallas_call(kernel, out_shape=(jax.ShapeDtypeStruct(leaf_rhs.shape, BF...  87.9 us
    pallas_call x1, Pallas kernels, body(): pl.pallas_call(copy_kernel, out_shape=tuple((jax.ShapeDtypeStruct(out.sha...  3.42 us

profile of v7, /device:TPU:1, one launch (start us, length us, event | category | flops | bytes accessed | tf_op | source)
XLA Modules:
  0.0 92.0 jit_solution(11232896742894470086)
XLA Ops:
  0.6 87.9 %shard_map.104 = (bf16[8,128,512]{2,1,0:T(8,128)(2,1)}, bf16[1,3,32,512]{3,2,1,0:T(8,128)(2,1)}) custom-call(s32[3,8]{1,0:T(4,128)} %bitcast.1, bf16[8,128,512]{2,1,0:T(8,128)(2,1)} %rhs_hbm.1, bf16[8,128,128]{2,1,0:T(8,128)(2,1)} %inverse_hbm.1, bf16[8,3,1024,128]{3,2,1,0:T(8,128)(2,1)} %couple_hbm.1, f32[8,128]{1,0:T(8,128)} %diag_hbm.1, ...), custom_call_target="tpu_custom_call" | custom-call | tf_op jit(solution)/shard_map/pallas_call | solution.py:838
  88.6 3.4 %shard_map.105 = (bf16[8,128,512]{2,1,0:T(8,128)(2,1)}, bf16[1,3,32,512]{3,2,1,0:T(8,128)(2,1)}) custom-call(bf16[8,128,512]{2,1,0:T(8,128)(2,1)} %get-tuple-element.4.leaf_ref, bf16[1,3,32,512]{3,2,1,0:T(8,128)(2,1)} %get-tuple-element.5.sep_ref), custom_call_target="tpu_custom_call" | custom-call | tf_op jit(solution)/shard_map/pallas_call | solution.py:861

commit v8 on v7

--- a/solution.py
+++ b/solution.py
@@ -311,6 +311,13 @@
     ).astype(BF16)
     mat0[y, x, core, :, 0:size] = unit_lower(own_inverse[...], first_row)
     mat0[y, x, core, :, size:] = beside
+    pl.semaphore_wait(barrier, len(peers))
+    mat_first(0)
+    local[2].wait()
+    local[3].wait()
+    mat_first(1)
+    mat_first(2)
+
     for i in range(4, 10):
         local[i].wait()
 
@@ -323,13 +330,6 @@
         return 0
 
     lax.fori_loop(0, blocks, solve_leaf, 0)
-
-    pl.semaphore_wait(barrier, len(peers))
-    mat_first(0)
-    local[2].wait()
-    local[3].wait()
-    mat_first(1)
-    mat_first(2)
 
     block_of = lax.broadcasted_iota(jnp.int32, (1, blocks * blk), 1) // blk
 
@@ -475,9 +475,9 @@
     two_slot = (layer % 4) // 2
 
     leaf_part(0)
+    mat_second(0)
     leaf_part(1)
     reduce_first(0)
-    mat_second(0)
     leaf_part(2)
     reduce_first(1)
     reduce_second(0)
@@ -485,7 +485,6 @@
     reduce_end(0)
     mat_third(0)
     reduce_second(1)
-    reduce_first(2)
     mat_second(2)
 
     @pl.when(is_one)
@@ -504,9 +503,9 @@
             is_one,
         )
 
+    reduce_first(2)
     reduce_end(1)
     mat_third(1)
-    reduce_second(2)
 
     @pl.when(is_one)
     def _():
@@ -523,8 +522,9 @@
             is_one,
         )
 
+    reduce_second(2)
+    mat_third(2)
     reduce_end(2)
-    mat_third(2)
 
     @pl.when(is_helper)
     def _():

time: 92.4 us -> 90.7 us (0.982)
  Pallas kernels: 91.3 us -> 89.2 us
    pallas_call x1, Pallas kernels: 87.9 us -> 85.8 us  [body(): pl.pallas_call(kernel, out_shape=(jax.ShapeDtypeStruct(leaf_rhs.shape, BF...]
where the time goes in v8:
time: 90.7 us; the launch traced here: 89.8 us
  Pallas kernels  89.2 us (98%)
    pallas_call x1, Pallas kernels, body(): pl.pallas_call(kernel, out_shape=(jax.ShapeDtypeStruct(leaf_rhs.shape, BF...  85.8 us
    pallas_call x1, Pallas kernels, body(): pl.pallas_call(copy_kernel, out_shape=tuple((jax.ShapeDtypeStruct(out.sha...  3.42 us

profile of v8, /device:TPU:1, one launch (start us, length us, event | category | flops | bytes accessed | tf_op | source)
XLA Modules:
  0.0 89.8 jit_solution(6683391529711259565)
XLA Ops:
  0.6 85.8 %shard_map.104 = (bf16[8,128,512]{2,1,0:T(8,128)(2,1)}, bf16[1,3,32,512]{3,2,1,0:T(8,128)(2,1)}) custom-call(s32[3,8]{1,0:T(4,128)} %bitcast.1, bf16[8,128,512]{2,1,0:T(8,128)(2,1)} %rhs_hbm.1, bf16[8,128,128]{2,1,0:T(8,128)(2,1)} %inverse_hbm.1, bf16[8,3,1024,128]{3,2,1,0:T(8,128)(2,1)} %couple_hbm.1, f32[8,128]{1,0:T(8,128)} %diag_hbm.1, ...), custom_call_target="tpu_custom_call" | custom-call | tf_op jit(solution)/shard_map/pallas_call | solution.py:838
  86.4 3.4 %shard_map.105 = (bf16[8,128,512]{2,1,0:T(8,128)(2,1)}, bf16[1,3,32,512]{3,2,1,0:T(8,128)(2,1)}) custom-call(bf16[8,128,512]{2,1,0:T(8,128)(2,1)} %get-tuple-element.4.leaf_ref, bf16[1,3,32,512]{3,2,1,0:T(8,128)(2,1)} %get-tuple-element.5.sep_ref), custom_call_target="tpu_custom_call" | custom-call | tf_op jit(solution)/shard_map/pallas_call | solution.py:861
